TPU v7x, 256 devices: a whole 4x4x8 slice. The times are simulated.
256 devices in a mesh: row: 32 (over x_lo, z, core), col: 8 (over x_hi, y).
Axes of the slice: x: 4 (x_hi: 2, x_lo: 2; x = x_hi * 2 + x_lo), y: 4, z: 8, core: 2. Of those that a mesh axis runs over, the one named last changes fastest.
Arguments:
- points: bfloat16 [98304, 64], P(('row', 'col')), may hold values from -6 to 6
- panel: bfloat16 [98304, 16], P(('row', 'col')), may hold values from -6 to 6
- tile_pairs: int32 [768, 768], P('row'), may hold values from 0 to 1, as said below
Outputs:
- applied: float32 [98304, 16], P(('row', 'col'))
Inputs may be any that keep to these rules, and one draw needn't show every extreme that they name: Each tile belongs to one of 6 clusters arranged in a cycle; tile_pairs[a, b] == 1 exactly when the clusters of tiles a and b are the same or neighbours in that cycle, so it is symmetric with ones on the diagonal.
All inputs are finite; a program needn't handle non-finite values.
Results may differ from a plain program's by a relative error of at most 0.0029.
Values may be sent and summed in bfloat16 or wider, within the bound.
A program may use at most 64 MiB of HBM per device.

v0:
```python
import jax
import jax.numpy as jnp
from jax import lax
from jax.sharding import PartitionSpec as P

D = 64
TILE = 128


def squares(values):
    floats = values.astype(jnp.float32)
    return jnp.sum(floats * floats, axis=1)


def local(points, panel, tile_pairs):
    per_dev = points.shape[0]
    col_count = lax.axis_size("col")
    row_place = lax.axis_index("row")
    col_place = lax.axis_index("col")
    row_x, row_v = (
        lax.all_gather(points, "col", axis=0, tiled=True),
        lax.all_gather(panel, "col", axis=0, tiled=True),
    )
    col_x, col_v = (
        lax.all_gather(points, "row", axis=0, tiled=True),
        lax.all_gather(panel, "row", axis=0, tiled=True),
    )
    row_norm = squares(row_x)
    col_norm = squares(col_x)
    row_total = row_x.shape[0]
    row_tiles = row_total // TILE
    row_ids = row_place * row_tiles + jnp.arange(row_tiles, dtype=jnp.int32)
    block_cols = 4 * per_dev
    direct = jnp.zeros((row_total, panel.shape[1]), jnp.float32)
    across = []
    for block in range(col_x.shape[0] // block_cols):
        start = block * block_cols
        col_ids = start + jnp.arange(block_cols, dtype=jnp.int32)
        tile_ids = (col_ids // per_dev * col_count + col_place) * (
            per_dev // TILE
        ) + col_ids % per_dev // TILE
        chosen = jnp.take(tile_pairs, tile_ids, axis=1) == 1
        lower = row_ids[:, None]
        higher = tile_ids[None, :]
        mine = lower <= higher
        weight = jnp.where(chosen & mine, jnp.where(lower == higher, 0.5, 1.0), 0.0)
        block_x = col_x[start : start + block_cols]
        block_v = col_v[start : start + block_cols]
        block_norm = col_norm[start : start + block_cols]

        def compute(block_x=block_x, block_v=block_v, block_norm=block_norm, weight=weight):
            cross = lax.dot_general(
                row_x, block_x, (((1,), (1,)), ((), ())), preferred_element_type=jnp.float32
            )
            dist = jnp.maximum(row_norm[:, None] + block_norm[None, :] - 2.0 * cross, 0.0)
            values = (
                jnp.exp(dist * (-2.0 / D)).reshape(row_tiles, TILE, block_cols) * weight[:, None, :]
            )
            kernel = values.reshape(row_total, block_cols).astype(jnp.bfloat16)
            forward = jnp.dot(kernel, block_v, preferred_element_type=jnp.float32)
            backward = lax.dot_general(
                kernel, row_v, (((0,), (0,)), ((), ())), preferred_element_type=jnp.float32
            )
            return (forward, backward)

        def skipped():
            return (
                jnp.zeros((row_total, panel.shape[1]), jnp.float32),
                jnp.zeros((block_cols, panel.shape[1]), jnp.float32),
            )

        forward, backward = lax.cond(jnp.any(weight > 0.0), compute, skipped)
        direct = direct + forward
        across.append(backward)
    applied = lax.psum_scatter(direct, "col", scatter_dimension=0, tiled=True)
    applied = applied + lax.psum_scatter(
        jnp.concatenate(across, axis=0), "row", scatter_dimension=0, tiled=True
    )
    return applied


def solution(mesh):
    in_specs = (P(("row", "col"), None), P(("row", "col"), None), P("row", None))
    out_specs = P(("row", "col"), None)
    return jax.shard_map(local, mesh=mesh, in_specs=in_specs, out_specs=out_specs, check_vma=False)
```

profile of v0, /device:TPU:8, one launch (start us, length us, event | category | flops | bytes accessed | tf_op | source)
XLA Modules:
  0.0 482.1 jit_solution(6048894501376439259)
XLA Ops:
  6.5 1.5 copy.5
  9.4 3.7 gather_fusion.2
  13.0 3.7 gather_fusion.4
  16.7 3.7 gather_fusion.5
  20.4 3.7 gather_fusion.6
  24.1 3.7 gather_fusion
  27.8 3.7 gather_fusion.1
  31.8 6.8 %compare_reduce_fusion.6 = (pred[]{:T(512)}, f32[24,1536]{0,1:T(8,128)}, pred[]{:T(512)}, f32[24,1536]{0,1:T(8,128)}, pred[]{:T(512)}, /*index=5*/f32[24,1536]{0...) fusion(s32[1536]{0:T(1024)S(1)} %get-tuple-element.323, ...), kind=kLoop, calls=%fused_computation.80 | loop fusion | flops 1990650 | bytes 1815654 | tf_op jit(solution)/shard_map/reduce_or | solution.py:72
  40.5 3.7 gather_fusion.3
  44.2 3.7 gather_fusion.7
  47.9 5.0 %compare_reduce_fusion.4 = (pred[]{:T(512)}, f32[24,1536]{0,1:T(8,128)}, pred[]{:T(512)}, f32[24,1536]{0,1:T(8,128)}) fusion(s32[1536]{0:T(1024)S(1)} %get-tuple-element.325, s32[24]{0:T(128)S(1)} %iota_add_fusion.7, s32[1536,24]{1,0:T(8,128)} %gather_fusion.3, pred[1536]{0:T(1024)(128)(4,1)S(1)} %get-tuple-element.334, s32[1536]{0:T(1024)S(1)} %get-tuple-element.329, ...), kind=kLoop, calls=%fused_computation.78 | loop fusion | flops 663550 | bytes 605282 | tf_op jit(solution)/shard_map/reduce_or | solution.py:72
  56.3 34.5 %all_gather.15 = bf16[3072,16]{0,1:T(8,128)(2,1)S(1)} all-gather(bf16[384,16]{0,1:T(8,128)(2,1)S(1)} %copy-done.7), channel_id=1, replica_groups=mesh['row'=32,'col'=8] {'col'}, dimensions={0}, use_global_device_ids=true | all-gather | bytes 110592 | tf_op jit(solution)/shard_map/all_gather | solution.py:22
  90.8 35.9 %all_gather.12 = bf16[3072,64]{1,0:T(8,128)(2,1)S(1)} all-gather(bf16[384,64]{1,0:T(8,128)(2,1)S(1)} %copy-done.3), channel_id=1, replica_groups=mesh['row'=32,'col'=8] {'col'}, dimensions={0}, use_global_device_ids=true | all-gather | bytes 442368 | tf_op jit(solution)/shard_map/all_gather | solution.py:21
  127.2 39.9 %all_gather.14 = bf16[12288,16]{0,1:T(8,128)(2,1)} all-gather(bf16[384,16]{0,1:T(8,128)(2,1)S(1)} %copy-done.7), channel_id=1, replica_groups=mesh['row'=32,'col'=8] {'row'}, dimensions={0}, use_global_device_ids=true | all-gather | bytes 405504 | tf_op jit(solution)/shard_map/all_gather | solution.py:26
  167.1 3.8 multiply_reduce_fusion
  170.9 13.6 %conditional.8 = (f32[3072,16]{0,1:T(8,128)S(1)}, f32[1536,16]{0,1:T(8,128)S(1)}) conditional(s32[]{:T(128)} %convert_element_type.54, () %tuple.70, (f32[3072]{0:T(1024)S(1)}, f32[12288]{0:T(1024)}, bf16[12288,64]{1,0:T(8,128)(2,1)}, bf16[3072,64]{1,0:T(8,128)(2,1)S(1)}, f32[24,1536]{0,1:T(8,128)}, /*index=5*/bf16[12288,16]{0,1:T(8,128)(2,1)}, ...), branch_computations={%region_3.5_spmd, %region_4.6_spmd} | conditional | flops 938999808 | bytes 30013456 | solution.py:72
  173.0 6.9 %fusion = bf16[3072,1536]{1,0:T(8,128)(2,1)S(1)} fusion(bf16[3072,64]{1,0:T(8,128)(2,1)S(1)} %get-tuple-element.144, f32[24,1536]{1,0:T(8,128)S(1)} %copy.7, f32[1536]{0:T(1024)S(1)} %slice.72, f32[3072]{0:T(1024)S(1)} %get-tuple-element.142, bf16[12288,64]{1,0:T(8,128)(2,1)} %get-tuple-element.145), kind=kOutput, calls=%fused_computation.9 | convolution fusion | flops 637009920 | bytes 10389504 | tf_op jit(solution)/shard_map/cond/branch_1_fun/dot_general | solution.py:52
  179.9 3.3 fusion.2
  185.2 15.5 %conditional.9 = (f32[3072,16]{0,1:T(8,128)}, f32[1536,16]{0,1:T(8,128)S(1)}) conditional(s32[]{:T(128)} %convert_element_type.57, () %tuple.72, (f32[3072]{0:T(1024)S(1)}, f32[12288]{0:T(1024)}, bf16[12288,64]{1,0:T(8,128)(2,1)}, bf16[3072,64]{1,0:T(8,128)(2,1)S(1)}, f32[24,1536]{0,1:T(8,128)}, /*index=5*/bf16[12288,16]{0,1:T(8,128)(2,1)}, ...), branch_computations={%region_6.8_spmd, %region_7.9_spmd} | conditional | flops 938999808 | bytes 30013456 | solution.py:72
  185.7 2.0 copy.9
  188.4 7.0 %fusion.4 = bf16[3072,1536]{1,0:T(8,128)(2,1)S(1)} fusion(bf16[3072,64]{1,0:T(8,128)(2,1)S(1)} %get-tuple-element.151, f32[24,1536]{1,0:T(8,128)} %copy.9, f32[1536]{0:T(1024)S(1)} %slice.75, f32[3072]{0:T(1024)S(1)} %get-tuple-element.149, bf16[12288,64]{1,0:T(8,128)(2,1)} %get-tuple-element.152), kind=kOutput, calls=%fused_computation.14 | convolution fusion | flops 637009920 | bytes 10389504 | tf_op jit(solution)/shard_map/cond/branch_1_fun/dot_general | solution.py:52
  195.4 4.0 fusion.6
  200.8 15.7 %conditional.10 = (f32[3072,16]{0,1:T(8,128)}, f32[1536,16]{0,1:T(8,128)}) conditional(s32[]{:T(128)} %convert_element_type.58, () %tuple.74, (f32[3072]{0:T(1024)S(1)}, f32[12288]{0:T(1024)}, bf16[12288,64]{1,0:T(8,128)(2,1)}, bf16[3072,64]{1,0:T(8,128)(2,1)S(1)}, f32[24,1536]{0,1:T(8,128)}, /*index=5*/bf16[12288,16]{0,1:T(8,128)(2,1)}, ...), branch_computations={%region_9.11_spmd, %region_10.12_spmd} | conditional | flops 938999808 | bytes 30013456 | solution.py:72
  200.8 2.0 copy.11
  203.5 7.0 %fusion.8 = bf16[3072,1536]{1,0:T(8,128)(2,1)S(1)} fusion(bf16[3072,64]{1,0:T(8,128)(2,1)S(1)} %get-tuple-element.158, f32[24,1536]{1,0:T(8,128)} %copy.11, f32[1536]{0:T(1024)S(1)} %slice.78, f32[3072]{0:T(1024)S(1)} %get-tuple-element.156, bf16[12288,64]{1,0:T(8,128)(2,1)} %get-tuple-element.159), kind=kOutput, calls=%fused_computation.19 | convolution fusion | flops 637009920 | bytes 10389504 | tf_op jit(solution)/shard_map/cond/branch_1_fun/dot_general | solution.py:52
  210.5 4.0 fusion.10
  214.5 2.0 fusion.142
  216.5 15.7 %conditional.11 = (f32[3072,16]{0,1:T(8,128)}, f32[1536,16]{0,1:T(8,128)}) conditional(s32[]{:T(128)} %convert_element_type.59, () %tuple.76, (f32[3072]{0:T(1024)S(1)}, f32[12288]{0:T(1024)}, bf16[12288,64]{1,0:T(8,128)(2,1)}, bf16[3072,64]{1,0:T(8,128)(2,1)S(1)}, f32[24,1536]{0,1:T(8,128)}, /*index=5*/bf16[12288,16]{0,1:T(8,128)(2,1)}, ...), branch_computations={%region_12.14_spmd, %region_13.15_spmd} | conditional | flops 938999808 | bytes 30013456 | solution.py:72
  216.5 2.0 copy.13
  219.2 7.0 %fusion.12 = bf16[3072,1536]{1,0:T(8,128)(2,1)S(1)} fusion(bf16[3072,64]{1,0:T(8,128)(2,1)S(1)} %get-tuple-element.165, f32[24,1536]{1,0:T(8,128)} %copy.13, f32[1536]{0:T(1024)S(1)} %slice.81, f32[3072]{0:T(1024)S(1)} %get-tuple-element.163, bf16[12288,64]{1,0:T(8,128)(2,1)} %get-tuple-element.166), kind=kOutput, calls=%fused_computation.24 | convolution fusion | flops 637009920 | bytes 10389504 | tf_op jit(solution)/shard_map/cond/branch_1_fun/dot_general | solution.py:52
  226.2 4.0 fusion.14
  230.2 2.0 fusion.143
  232.2 13.4 %conditional.12 = (f32[3072,16]{0,1:T(8,128)S(1)}, f32[1536,16]{0,1:T(8,128)S(1)}) conditional(s32[]{:T(128)} %convert_element_type.60, () %tuple.78, (f32[3072]{0:T(1024)S(1)}, f32[12288]{0:T(1024)}, bf16[12288,64]{1,0:T(8,128)(2,1)}, bf16[3072,64]{1,0:T(8,128)(2,1)S(1)}, f32[24,1536]{0,1:T(8,128)S(1)}, /*index=5*/bf16[12288,16]{0,1:T(8,128)(2,1)}, ...), branch_computations={%region_15.17_spmd, %region_16.18_spmd} | conditional | flops 938999808 | bytes 30013456 | solution.py:72
  233.9 7.0 %fusion.16 = bf16[3072,1536]{1,0:T(8,128)(2,1)S(1)} fusion(bf16[3072,64]{1,0:T(8,128)(2,1)S(1)} %get-tuple-element.172, f32[24,1536]{1,0:T(8,128)} %copy.15, f32[1536]{0:T(1024)S(1)} %slice.84, f32[3072]{0:T(1024)S(1)} %get-tuple-element.170, bf16[12288,64]{1,0:T(8,128)(2,1)} %get-tuple-element.173), kind=kOutput, calls=%fused_computation.29 | convolution fusion | flops 637009920 | bytes 10389504 | tf_op jit(solution)/shard_map/cond/branch_1_fun/dot_general | solution.py:52
  240.9 3.3 fusion.18
  246.2 12.5 %conditional.13 = (f32[3072,16]{0,1:T(8,128)S(1)}, f32[1536,16]{0,1:T(8,128)S(1)}) conditional(s32[]{:T(128)} %convert_element_type.61, () %tuple.80, (f32[3072]{0:T(1024)S(1)}, f32[12288]{0:T(1024)}, bf16[12288,64]{1,0:T(8,128)(2,1)}, bf16[3072,64]{1,0:T(8,128)(2,1)S(1)}, f32[24,1536]{0,1:T(8,128)S(1)}, /*index=5*/bf16[12288,16]{0,1:T(8,128)(2,1)}, ...), branch_computations={%region_18.20_spmd, %region_19.21_spmd} | conditional | flops 938999808 | bytes 30013456 | solution.py:72
  247.2 6.9 %fusion.20 = bf16[3072,1536]{1,0:T(8,128)(2,1)S(1)} fusion(bf16[3072,64]{1,0:T(8,128)(2,1)S(1)} %get-tuple-element.179, f32[24,1536]{1,0:T(8,128)S(1)} %copy.17, f32[1536]{0:T(1024)S(1)} %slice.87, f32[3072]{0:T(1024)S(1)} %get-tuple-element.177, bf16[12288,64]{1,0:T(8,128)(2,1)} %get-tuple-element.180), kind=kOutput, calls=%fused_computation.34 | convolution fusion | flops 637009920 | bytes 10389504 | tf_op jit(solution)/shard_map/cond/branch_1_fun/dot_general | solution.py:52
  254.0 3.3 fusion.22
  259.4 12.5 %conditional.14 = (f32[3072,16]{0,1:T(8,128)S(1)}, f32[1536,16]{0,1:T(8,128)S(1)}) conditional(s32[]{:T(128)} %convert_element_type.62, () %tuple.82, (f32[3072]{0:T(1024)S(1)}, f32[12288]{0:T(1024)}, bf16[12288,64]{1,0:T(8,128)(2,1)}, bf16[3072,64]{1,0:T(8,128)(2,1)S(1)}, f32[24,1536]{0,1:T(8,128)S(1)}, /*index=5*/bf16[12288,16]{0,1:T(8,128)(2,1)}, ...), branch_computations={%region_21.23_spmd, %region_22.24_spmd} | conditional | flops 938999808 | bytes 30013456 | solution.py:72
  260.3 6.9 %fusion.24 = bf16[3072,1536]{1,0:T(8,128)(2,1)S(1)} fusion(bf16[3072,64]{1,0:T(8,128)(2,1)S(1)} %get-tuple-element.186, f32[24,1536]{1,0:T(8,128)S(1)} %copy.19, f32[1536]{0:T(1024)S(1)} %slice.90, f32[3072]{0:T(1024)S(1)} %get-tuple-element.184, bf16[12288,64]{1,0:T(8,128)(2,1)} %get-tuple-element.187), kind=kOutput, calls=%fused_computation.39 | convolution fusion | flops 637009920 | bytes 10389504 | tf_op jit(solution)/shard_map/cond/branch_1_fun/dot_general | solution.py:52
  267.2 3.3 fusion.26
  272.5 13.3 %conditional.15 = (f32[3072,16]{0,1:T(8,128)S(1)}, f32[1536,16]{0,1:T(8,128)}) conditional(s32[]{:T(128)} %convert_element_type.63, () %tuple.84, (f32[3072]{0:T(1024)S(1)}, f32[12288]{0:T(1024)}, bf16[12288,64]{1,0:T(8,128)(2,1)}, bf16[3072,64]{1,0:T(8,128)(2,1)S(1)}, f32[24,1536]{0,1:T(8,128)S(1)}, /*index=5*/bf16[12288,16]{0,1:T(8,128)(2,1)}, ...), branch_computations={%region_24.26_spmd, %region_25.27_spmd} | conditional | flops 938999808 | bytes 30013456 | solution.py:72
  273.6 6.9 %fusion.28 = bf16[3072,1536]{1,0:T(8,128)(2,1)S(1)} fusion(bf16[3072,64]{1,0:T(8,128)(2,1)S(1)} %get-tuple-element.193, f32[24,1536]{1,0:T(8,128)S(1)} %copy.21, f32[1536]{0:T(1024)S(1)} %slice.93, f32[3072]{0:T(1024)S(1)} %get-tuple-element.191, bf16[12288,64]{1,0:T(8,128)(2,1)} %get-tuple-element.194), kind=kOutput, calls=%fused_computation.44 | convolution fusion | flops 637009920 | bytes 10389504 | tf_op jit(solution)/shard_map/cond/branch_1_fun/dot_general | solution.py:52
  280.5 3.3 fusion.30
  283.8 2.0 fusion.147
  285.8 1.9 add_add_fusion
  294.1 61.6 %reduce-scatter.3.cloned.1.call-done = f32[384,16]{0,1:T(8,128)} async-done(((f32[3072,16]{0,1:T(8,128)}), f32[384,16]{0,1:T(8,128)}) %reduce-scatter.3.cloned.1.call-update) | async-done | bytes 24592 | tf_op jit(solution)/shard_map/reduce_scatter | solution.py:75
  355.7 118.3 %reduce-scatter.5.cloned.1.call-done = f32[384,16]{0,1:T(8,128)} async-done(((f32[12288,16]{0,1:T(8,128)}), f32[384,16]{0,1:T(8,128)}) %reduce-scatter.5.cloned.1.call-update) | async-done | bytes 24592 | tf_op jit(solution)/shard_map/reduce_scatter | solution.py:76
  (73 shorter events, 27.6 us)
Async XLA Ops:
  6.5 160.6 %all-gather.2.cloned.1.call-start = ((), (), s32[]{:S(2)}) async-start(), calls=%async_computation.2 | async-start | bytes 3244032 | tf_op jit(solution)/shard_map/all_gather | solution.py:25
  8.1 347.6 %reduce-scatter.3.cloned.1.call-start = ((), (), s32[]{:S(2)}) async-start(), calls=%async_computation.3 | async-start | bytes 221184 | tf_op jit(solution)/shard_map/reduce_scatter | solution.py:75
  24.1 32.2 %copy-start.7 = (bf16[384,16]{0,1:T(8,128)(2,1)S(1)}, bf16[384,16]{0,1:T(8,128)(2,1)}, u32[]{:S(2)}) copy-start(bf16[384,16]{0,1:T(8,128)(2,1)} %param.22) | copy-start | bytes 36868
  24.1 66.7 %copy-start.3 = (bf16[384,64]{1,0:T(8,128)(2,1)S(1)}, bf16[384,64]{1,0:T(8,128)(2,1)}, u32[]{:S(2)}) copy-start(bf16[384,64]{1,0:T(8,128)(2,1)} %copy.5) | copy-start | bytes 147460
  245.6 0.6 copy-start.4
  258.7 0.6 copy-start.5
  258.7 13.1 %copy-start = (f32[24,1536]{0,1:T(8,128)S(1)}, f32[24,1536]{0,1:T(8,128)}, u32[]{:S(2)}) copy-start(f32[24,1536]{0,1:T(8,128)} %get-tuple-element.313) | copy-start | bytes 442372
  271.8 0.7 copy-start.6
  271.8 15.9 %copy-start.1 = (f32[12288,16]{0,1:T(8,128)S(1)}, f32[12288,16]{0,1:T(8,128)}, u32[]{:S(2)}) copy-start(f32[12288,16]{0,1:T(8,128)} %constant_dynamic-update-slice_fusion.7) | copy-start | bytes 2359300
  287.7 186.3 %reduce-scatter.5.cloned.1.call-start = ((), (), s32[]{:S(2)}) async-start(), calls=%async_computation.4 | async-start | bytes 811008 | tf_op jit(solution)/shard_map/reduce_scatter | solution.py:76
  293.2 0.9 copy-start.2
Sparse Core Ops, SparseCore 0:
  9.2 69.0 all-gather.1
  287.8 67.8 reduce-scatter.2
  358.4 115.5 reduce-scatter.4
where the time goes:
time: 491 us; the launch traced here: 482 us
  waiting for transfers between devices  180 us (37%)
  blocking collectives  110 us (22%)
  matrix products  96.6 us (20%)
  local copies, waits for them, and re-layouts  55.7 us (11%)
  other arithmetic  19.8 us (4%)
  between operations  18.7 us (4%)
    reduce_scatter x1, waiting for transfers between devices, local(): lax.psum_scatter(jnp.concatenate(across, axis=0), 'row', scatter_dimensio...  118 us
    reduce_scatter x1, waiting for transfers between devices, local(): applied = lax.psum_scatter(direct, 'col', scatter_dimension=0, tiled=True)  61.6 us
    dot_general x8, matrix products, compute(): lax.dot_general(row_x, block_x, (((1,), (1,)), ((), ())), preferred_eleme...  55.3 us
    all_gather x1, blocking collectives, local(): lax.all_gather(panel, 'row', axis=0, tiled=True)  39.9 us
    all_gather x1, blocking collectives, local(): lax.all_gather(points, 'col', axis=0, tiled=True)  35.9 us
    all_gather x1, blocking collectives, local(): lax.all_gather(panel, 'col', axis=0, tiled=True)  34.5 us
    gather x8, local copies, waits for them, and re-layouts, local(): chosen = jnp.take(tile_pairs, tile_ids, axis=1) == 1  29.4 us
    dot_general x8, matrix products, compute(): forward = jnp.dot(kernel, block_v, preferred_element_type=jnp.float32)  28.7 us
  transfers between devices with their start and end apart: 3, of which 2 were waited for; matrix products, arithmetic and copies ran while one was open for 10% of the time, Pallas kernels for 0%

commit v1 on v0

v1 whole, which is shorter than its diff:
```python
import jax
import jax.numpy as jnp
from jax import lax
from jax.experimental import pallas as pl
from jax.experimental.pallas import tpu as pltpu
from jax.sharding import PartitionSpec as P

D = 64
PW = 16
TILE = 128
BLK = 384
NX, NY, NZ = 4, 4, 8
PLANE = NX * NY * 2
CT = 3 * PLANE
RT = 3 * NZ
PAIRS = RT // 2
BIG = 9984.0
F32, BF16 = jnp.float32, jnp.bfloat16
MESH = pl.DeviceIdType.MESH
VMEM = pl.BlockSpec(memory_space=pltpu.VMEM)
SMEM = pl.BlockSpec(memory_space=pltpu.SMEM)


def place():
    row, col = lax.axis_index("row"), lax.axis_index("col")
    x = (col // 4) * 2 + row // 16
    return x, col % 4, (row // 2) % 8, row % 2


def device(x, y, z, core):
    return ((x % 2) * 16 + z * 2 + core, (x // 2) * 4 + y)


def slot_of(x, y, core):
    return (x % 2) * 16 + core * 8 + (x // 2) * 4 + y


def iota(shape, dim):
    return lax.broadcasted_iota(jnp.int32, shape, dim)


def norm_parts(x_t):
    floats = x_t.astype(F32)
    n = jnp.sum(floats * floats, axis=0, keepdims=True) * (-1.0 / 32.0)
    hi = n.astype(BF16).astype(F32)
    rest = n - hi
    mid = rest.astype(BF16).astype(F32)
    return hi, mid, rest - mid


def mix(rows, first, hi, mid, lo, other):
    one = jnp.where((rows >= other) & (rows < other + 3), 1.0, 0.0)
    return jnp.where(rows == first, hi, jnp.where(rows == first + 1, mid, jnp.where(rows == first + 2, lo, one)))


def lists_of(m, list_ref, info_ref):
    gram = lax.dot_general(m, m, (((1,), (1,)), ((), ())), preferred_element_type=F32)
    sub, lane = iota((RT, RT), 0), iota((RT, RT), 1)
    eye = sub == lane
    n_col = jnp.sum(m, axis=1, keepdims=True)
    n_row = jnp.sum(jnp.where(eye, gram, 0.0), axis=0, keepdims=True)
    apart = n_col + n_row - 2.0 * gram

    def key_of(overlap, apart0, ids, axis):
        score = jnp.where(apart0 > 0.5, overlap * 32.0 - ids.astype(F32), -1e6)
        return score == jnp.max(score, axis=axis, keepdims=True)

    o_row, a_row = gram[0:1, :], apart[0:1, :]
    o_col, a_col = gram[:, 0:1], apart[:, 0:1]
    e_row = key_of(o_row, a_row, lane[0:1, :], 1)
    e_col = key_of(o_col, a_col, sub[:, 0:1], 0)
    p_col = jnp.sum(jnp.where(e_row, gram, 0.0), axis=1, keepdims=True)
    p_row = jnp.sum(jnp.where(e_col, gram, 0.0), axis=0, keepdims=True)

    def order(o, p, a):
        return jnp.where(a < 0.5, 0.0, jnp.where(p > o, 1e4 - o, 2e4 + o))

    k_row, k_col = order(o_row, p_row, a_row), order(o_col, p_col, a_col)
    before = (k_col < k_row) | ((k_col == k_row) & (sub < lane))
    rank = jnp.sum(before.astype(F32), axis=0, keepdims=True)
    pair = iota((16, RT), 0).astype(F32)
    even = jnp.where(rank == 2.0 * pair, 1.0, 0.0)
    odd = jnp.where(rank == 2.0 * pair + 1.0, 1.0, 0.0)
    both = jnp.maximum(
        jnp.dot(even, m, preferred_element_type=F32), jnp.dot(odd, m, preferred_element_type=F32)
    )
    tri = jnp.where(iota((128, 128), 0) < iota((128, 128), 1), 1.0, 0.0)
    pos = jnp.dot(both, tri, preferred_element_type=F32)
    count = jnp.sum(both, axis=1, keepdims=True)
    where = jnp.where(both > 0.5, pos, -1.0)
    ids = iota((16, 128), 1)
    k = iota((128, 128), 0).astype(F32)
    prow = iota((16, 128), 0)
    total = jnp.where(ids.astype(F32) >= count, float(CT), 0.0)
    for p in range(PAIRS):
        hit = jnp.where(where[p : p + 1, :] == k, 1.0, 0.0)
        got = lax.dot_general(ids.astype(F32), hit, (((1,), (1,)), ((), ())), preferred_element_type=F32)
        total = total + jnp.where(prow == p, got, 0.0)
    list_ref[...] = total.astype(jnp.int32)
    t = iota((16, RT), 1).astype(F32)
    first = jnp.sum(even * t, axis=1, keepdims=True)
    second = jnp.sum(odd * t, axis=1, keepdims=True)
    info = jnp.where(ids == 0, first, jnp.where(ids == 1, second, jnp.where(ids == 2, count, 0.0)))
    info_ref[...] = info.astype(jnp.int32)


def gather_kernel(
    pts, pan, tp, xj, vj, xi, lists, info, own, colbuf, rowbuf, mask, psend, precv, fsend, frecv, zsend, zrecv
):
    x, y, z, core = place()
    c = (x // 2) * 4 + y
    me = slot_of(x, y, core)

    def peer(o):
        return (x + o // 4) % 4, (y + o % 4) % 4

    barrier = pltpu.get_barrier_semaphore()
    for o in range(1, 16):
        px, py = peer(o)
        pl.semaphore_signal(barrier, inc=1, device_id=device(px, py, z, core), device_id_type=MESH)
    for o in range(1, NZ):
        pl.semaphore_signal(barrier, inc=1, device_id=device(x, y, (z + o) % NZ, core), device_id_type=MESH)
    pl.semaphore_signal(barrier, inc=1, device_id=device(x, y, z, 1 - core), device_id_type=MESH)

    own[0:D, :] = pts[...].astype(F32).T.astype(BF16)
    own[D : D + PW, :] = pan[...].astype(F32).T.astype(BF16)
    r, t = iota((16, 24), 0), iota((16, 24), 1)
    flags = tp[...].astype(F32)
    pick0 = jnp.where((r < 3) & (t == 3 * c + r), 1.0, 0.0)
    pick1 = jnp.where((r >= 3) & (r < 6) & (t == 3 * c + r - 3), 1.0, 0.0)
    own[D + PW : D + PW + 16, :] = (
        jnp.dot(pick0, flags[:, :BLK], preferred_element_type=F32)
        + jnp.dot(pick1, flags[:, BLK:], preferred_element_type=F32)
    ).astype(BF16)
    pl.semaphore_wait(barrier, 15 + NZ - 1 + 1)

    def plane_copy(o):
        px, py = peer(o)
        return pltpu.make_async_remote_copy(
            src_ref=own.at[0 : D + PW],
            dst_ref=colbuf.at[me],
            send_sem=psend.at[o],
            recv_sem=precv.at[me],
            device_id=device(px, py, z, core),
            device_id_type=MESH,
        )

    def z_copy(o):
        return pltpu.make_async_remote_copy(
            src_ref=own,
            dst_ref=rowbuf.at[z],
            send_sem=zsend.at[o],
            recv_sem=zrecv.at[z],
            device_id=device(x, y, (z + o) % NZ, core),
            device_id_type=MESH,
        )

    def fwd_copy(slot, src):
        return pltpu.make_async_remote_copy(
            src_ref=src,
            dst_ref=colbuf.at[slot],
            send_sem=fsend.at[slot],
            recv_sem=frecv.at[slot],
            device_id=device(x, y, z, 1 - core),
            device_id_type=MESH,
        )

    near = (1, 3, 4, 12, 2, 8, 5, 7, 13, 15, 6, 14, 9, 11, 10)
    z_near = (1, 7, 2, 6, 3, 5, 4)
    for o in z_near:
        z_copy(o).start()
    for o in near:
        plane_copy(o).start()
    fwd_copy(me, own.at[0 : D + PW]).start()

    rowbuf[z] = own[...]
    colbuf[me] = own[0 : D + PW, :]
    xj[CT] = jnp.zeros((TILE, TILE), BF16)
    vj[CT] = jnp.zeros((PW, TILE), BF16)

    lane = iota((BLK, 128), 1)
    pos = iota((BLK, 128), 0) - 48 * z
    shift0 = jnp.where((lane < 48) & (pos == lane), 1.0, 0.0)
    shift1 = jnp.where((lane >= 48) & (lane < 96) & (pos == lane - 48), 1.0, 0.0)
    mask[...] = jnp.zeros((RT, 128), F32)
    row64 = iota((64, TILE), 0)
    for o in (0,) + z_near:
        zz = (z + o) % NZ
        if o:
            pltpu.make_async_remote_copy(
                src_ref=own,
                dst_ref=rowbuf.at[zz],
                send_sem=zsend.at[o],
                recv_sem=zrecv.at[zz],
                device_id=device(x, y, zz, core),
                device_id_type=MESH,
            ).wait_recv()
        block = rowbuf[zz]
        hi, mid, lo = norm_parts(block[0:D, :])
        for q in range(3):
            at = slice(q * TILE, (q + 1) * TILE)
            tail = mix(row64, 0, hi[:, at], mid[:, at], lo[:, at], 3)
            tail = jnp.where(row64 == 8 + 3 * zz + q, 1.0, tail)
            xi[3 * zz + q, 0:D, :] = block[0:D, at] * jnp.bfloat16(1.0 / 16.0)
            xi[3 * zz + q, D:128, :] = tail.astype(BF16)
        flag = block[D + PW :, :].astype(F32)
        got0 = jnp.dot(flag, shift0, preferred_element_type=F32)
        got1 = jnp.dot(flag, shift1, preferred_element_type=F32)
        mine = iota((RT, 16), 0) - 3 * zz
        src = iota((RT, 16), 1)
        put0 = jnp.where((mine >= 0) & (mine < 3) & (src == mine), 1.0, 0.0)
        put1 = jnp.where((mine >= 0) & (mine < 3) & (src == mine + 3), 1.0, 0.0)
        mask[...] += jnp.dot(put0, got0, preferred_element_type=F32) + jnp.dot(
            put1, got1, preferred_element_type=F32
        )
    lists_of(mask[...], lists, info)

    def column(slot):
        block = colbuf[slot]
        hi, mid, lo = norm_parts(block[0:D, :])
        lanes = iota((RT, 128), 1)
        for q in range(3):
            at = slice(q * TILE, (q + 1) * TILE)
            tail = mix(row64[0:8], 3, hi[:, at], mid[:, at], lo[:, at], 0)
            on = jnp.sum(jnp.where(lanes == 3 * slot + q, mask[...], 0.0), axis=1, keepdims=True)
            off = jnp.broadcast_to((on - 1.0) * BIG, (RT, TILE))
            feats = jnp.concatenate(
                [block[0:D, at].astype(F32), tail, off, jnp.zeros((128 - D - 8 - RT, TILE), F32)], axis=0
            )
            xj[3 * slot + q] = feats.T.astype(BF16)
            vj[3 * slot + q] = block[D:, at]

    column(me)

    def arrive(o):
        px, py = peer(o)
        slot = slot_of(px, py, core)
        pltpu.make_async_remote_copy(
            src_ref=own.at[0 : D + PW],
            dst_ref=colbuf.at[slot],
            send_sem=psend.at[o],
            recv_sem=precv.at[slot],
            device_id=device(px, py, z, core),
            device_id_type=MESH,
        ).wait_recv()
        fwd_copy(slot, colbuf.at[slot]).start()
        return slot

    for o in near:
        column(arrive(o))
    for o in (0,) + near:
        px, py = peer(o)
        slot = slot_of(px, py, 1 - core)
        fwd_copy(slot, colbuf.at[slot]).wait_recv()
        column(slot)
    for o in z_near:
        z_copy(o).wait_send()
    for o in near:
        plane_copy(o).wait_send()
    for o in (0,) + near:
        px, py = peer(o)
        slot = slot_of(px, py, core)
        fwd_copy(slot, colbuf.at[slot]).wait_send()


JT = 4
SUB = 4


def apply_kernel(lists, info, xj, vj, xi, out, *held):
    out[...] = jnp.zeros_like(out)

    def compute(p, k, held_ref):
        w = jnp.concatenate([xi[info[p, 0]], xi[info[p, 1]]], axis=1)
        a = jnp.concatenate([xj[lists[p, k + q]] for q in range(JT)], axis=0)
        s = jnp.dot(a, w, preferred_element_type=F32)
        held_ref[...] = jnp.exp(jnp.minimum(s, 0.0)).astype(BF16)

    def apply(p, k, held_ref):
        v = jnp.concatenate([vj[lists[p, k + q]] for q in range(JT)], axis=1)
        r = jnp.dot(v, held_ref[...], preferred_element_type=F32)
        a, b = info[p, 0], info[p, 1]
        out[a] += r[:, :TILE]
        out[b] += r[:, TILE:]

    def following(p, k):
        end = k + JT >= info[p, 2]
        last = p == PAIRS - 1
        k = jnp.where(end, jnp.where(last, 100, 0), k + JT)
        return jnp.where(end & ~last, p + 1, p), k

    total = sum(jnp.maximum((info[p, 2] + JT - 1) // JT, 1) for p in range(PAIRS))
    zero = jnp.int32(0)
    compute(zero, zero, held[SUB - 1])

    def step(_, at):
        for u in range(SUB):
            nxt = following(*at)
            compute(*nxt, held[u])
            apply(*at, held[u - 1])
            at = nxt
        return at

    lax.fori_loop(0, (total + SUB - 1) // SUB, step, (zero, zero))


def reduce_kernel(part, out, got, send, recv):
    x, y, z, core = place()
    barrier = pltpu.get_barrier_semaphore()
    for o in range(1, NZ):
        pl.semaphore_signal(barrier, inc=1, device_id=device(x, y, (z + o) % NZ, core), device_id_type=MESH)
    pl.semaphore_wait(barrier, NZ - 1)

    def copy(o, slot):
        to = (z + o) % NZ
        return pltpu.make_async_remote_copy(
            src_ref=part.at[pl.ds(3 * to, 3)],
            dst_ref=got.at[slot],
            send_sem=send.at[o],
            recv_sem=recv.at[slot],
            device_id=device(x, y, to, core),
            device_id_type=MESH,
        )

    for o in (4, 3, 5, 2, 6, 1, 7):
        copy(o, z).start()
    total = [part[3 * z + q] for q in range(3)]
    for o in (1, 7, 2, 6, 3, 5, 4):
        zz = (z + o) % NZ
        copy(o, zz).wait_recv()
        total = [total[q] + got[zz, q] for q in range(3)]
    for q in range(3):
        out[q * TILE : (q + 1) * TILE, :] = total[q].T
    for o in range(1, NZ):
        copy(o, z).wait_send()


def local(points, panel, tile_pairs):
    shape = jax.ShapeDtypeStruct
    dma = pltpu.SemaphoreType.DMA
    xj, vj, xi, lists, info = pl.pallas_call(
        gather_kernel,
        out_shape=(
            shape((CT + 1, TILE, TILE), BF16),
            shape((CT + 1, PW, TILE), BF16),
            shape((RT, TILE, TILE), BF16),
            shape((16, 128), jnp.int32),
            shape((16, 128), jnp.int32),
        ),
        in_specs=[VMEM] * 3,
        out_specs=[VMEM] * 5,
        scratch_shapes=[
            pltpu.VMEM((D + PW + 16, BLK), BF16),
            pltpu.VMEM((PLANE, D + PW, BLK), BF16),
            pltpu.VMEM((NZ, D + PW + 16, BLK), BF16),
            pltpu.VMEM((RT, 128), F32),
            dma((16,)),
            dma((PLANE,)),
            dma((PLANE,)),
            dma((PLANE,)),
            dma((NZ,)),
            dma((NZ,)),
        ],
        compiler_params=pltpu.CompilerParams(
            collective_id=0, has_side_effects=True, vmem_limit_bytes=40 * 2**20
        ),
        name="gather",
    )(points, panel, tile_pairs)
    part = pl.pallas_call(
        apply_kernel,
        out_shape=shape((RT, PW, TILE), F32),
        in_specs=[SMEM, SMEM, VMEM, VMEM, VMEM],
        out_specs=VMEM,
        scratch_shapes=[pltpu.VMEM((JT * TILE, 2 * TILE), BF16)] * SUB,
        compiler_params=pltpu.CompilerParams(vmem_limit_bytes=40 * 2**20),
        name="apply",
    )(lists, info, xj, vj, xi)
    return pl.pallas_call(
        reduce_kernel,
        out_shape=shape((BLK, PW), F32),
        in_specs=[VMEM],
        out_specs=VMEM,
        scratch_shapes=[pltpu.VMEM((NZ, 3, PW, TILE), F32), dma((NZ,)), dma((NZ,))],
        compiler_params=pltpu.CompilerParams(
            collective_id=1, has_side_effects=True, vmem_limit_bytes=40 * 2**20
        ),
        name="reduce",
    )(part)


def solution(mesh):
    in_specs = (P(("row", "col"), None), P(("row", "col"), None), P("row", None))
    out_specs = P(("row", "col"), None)
    return jax.shard_map(local, mesh=mesh, in_specs=in_specs, out_specs=out_specs, check_vma=False)
```

time: 491 us -> 75.1 us (0.15); the launches traced: 482 us -> 74.9 us
  waiting for transfers between devices: 180 us -> 0 us
  blocking collectives: 110 us -> 0 us
  matrix products: 96.6 us -> 0 us
  Pallas kernels: 0 us -> 71.5 us
  local copies, waits for them, and re-layouts: 55.7 us -> 3.34 us
  other arithmetic: 19.8 us -> 0 us
  between operations: 18.7 us -> 0.03 us
    reduce_scatter x2 -> x0, waiting for transfers between devices: 180 us -> none  [the longest x1 118 us: local(): lax.psum_scatter(jnp.concatenate(across, axis=0), 'row', scatter_dimensio...]
    all_gather x3 -> x0, blocking collectives: 110 us -> none  [the longest x1 39.9 us: local(): lax.all_gather(panel, 'row', axis=0, tiled=True)]
    dot_general x24 -> x0, matrix products: 96.6 us -> none  [the longest x8 55.3 us: compute(): lax.dot_general(row_x, block_x, (((1,), (1,)), ((), ())), preferred_eleme...]
    pallas_call x0 -> x3, Pallas kernels: none -> 71.5 us  [the longest x1 32.8 us: local(): pl.pallas_call(gather_kernel, out_shape=(shape((CT + 1, TILE, TILE), BF16...]
    gather x8 -> x0, local copies, waits for them, and re-layouts: 29.4 us -> none  [local(): chosen = jnp.take(tile_pairs, tile_ids, axis=1) == 1]
    reduce_or x2 -> x0, other arithmetic: 11.9 us -> none  [local(): forward, backward = lax.cond(jnp.any(weight > 0.0), compute, skipped)]
    another operation x8 -> x0, local copies, waits for them, and re-layouts: 9.09 us -> none
    unnamed x25 -> x4, local copies, waits for them, and re-layouts: 10.6 us -> 2.62 us
  transfers between devices with their start and end apart: 3 -> 0, of which waited for: 2 -> 0; matrix products, arithmetic and copies ran while one was open for 10% -> 0% of each run, Pallas kernels for 0% -> 0%
where the time goes in v1:
time: 75.1 us; the launch traced here: 74.9 us
  Pallas kernels  71.5 us (95%)
  local copies, waits for them, and re-layouts  3.34 us (4%)
    pallas_call x1, Pallas kernels, local(): pl.pallas_call(gather_kernel, out_shape=(shape((CT + 1, TILE, TILE), BF16...  32.8 us
    pallas_call x1, Pallas kernels, local(): pl.pallas_call(apply_kernel, out_shape=shape((RT, PW, TILE), F32), in_spe...  28.6 us
    pallas_call x1, Pallas kernels, local(): pl.pallas_call(reduce_kernel, out_shape=shape((BLK, PW), F32), in_specs=[...  10.1 us
    unnamed x4, local copies, waits for them, and re-layouts  2.62 us

profile of v1, /device:TPU:8, one launch (start us, length us, event | category | flops | bytes accessed | tf_op | source)
XLA Modules:
  0.0 74.9 jit_solution(11458420142022336615)
XLA Ops:
  0.0 0.9 %copy.4.pts = bf16[384,64]{1,0:T(8,128)(2,1)S(1)} copy(bf16[384,64]{0,1:T(8,128)(2,1)} %param.3) | data formatting | bytes 98304 | tf_op args[0]
  0.9 0.8 %copy.5.pan = bf16[384,16]{1,0:T(8,128)(2,1)S(1)} copy(bf16[384,16]{0,1:T(8,128)(2,1)} %param.4) | data formatting | bytes 24576 | tf_op args[1]
  1.8 0.0 copy-start
  1.8 0.9 %copy-done = s32[24,768]{1,0:T(8,128)S(1)} copy-done((s32[24,768]{1,0:T(8,128)S(1)}, s32[24,768]{1,0:T(8,128)}, u32[]{:S(2)}) %copy-start) | copy-done | bytes 73752
  2.6 32.8 %gather.1 = (bf16[97,128,128]{2,1,0:T(8,128)(2,1)S(1)}, bf16[97,16,128]{2,1,0:T(8,128)(2,1)S(1)}, bf16[24,128,128]{2,1,0:T(8,128)(2,1)S(1)}, s32[16,128]{1,0:T(8,128)S(1)}, s32[16,128]{1,0:T(8,128)S(1)}) custom-call(bf16[384,64]{1,0:T(8,128)(2,1)S(1)} %copy.4.pts, bf16[384,16]{1,0:T(8,128)(2,1)S(1)} %copy.5.pan, s32[24,768]{1,0:T(8,128)S(1)} %copy-done), custom_call_target="tpu_custom_call" | custom-call | tf_op jit(solution)/shard_map/gather/pallas_call | solution.py:341
  35.4 28.6 %apply.1.part = f32[24,16,128]{2,1,0:T(8,128)S(1)} custom-call(s32[16,128]{1,0:T(8,128)S(1)} %get-tuple-element.10.lists, s32[16,128]{1,0:T(8,128)S(1)} %get-tuple-element.11.info, bf16[97,128,128]{2,1,0:T(8,128)(2,1)S(1)} %get-tuple-element.12.xj, bf16[97,16,128]{2,1,0:T(8,128)(2,1)S(1)} %get-tuple-element.13.vj, bf16[24,128,128]{2,1,0:T(8,128)(2,1)S(1)} %get-tuple-element.14.xi), custom_call_target="tpu_custom_call" | custom-call | tf_op jit(solution)/shard_map/apply/pallas_call | solution.py:369
  64.1 10.1 %reduce.1 = f32[384,16]{1,0:T(8,128)S(1)} custom-call(f32[24,16,128]{2,1,0:T(8,128)S(1)} %apply.1.part), custom_call_target="tpu_custom_call" | custom-call | tf_op jit(solution)/shard_map/reduce/pallas_call | solution.py:378
  74.2 0.7 copy.6
Async XLA Ops:
  1.8 0.9 %copy-start = (s32[24,768]{1,0:T(8,128)S(1)}, s32[24,768]{1,0:T(8,128)}, u32[]{:S(2)}) copy-start(s32[24,768]{1,0:T(8,128)} %tp.1) | copy-start | bytes 221188

commit v2 on v1

v2 whole, which is shorter than its diff:
```python
import jax
import jax.numpy as jnp
from jax import lax
from jax.experimental import pallas as pl
from jax.experimental.pallas import tpu as pltpu
from jax.sharding import PartitionSpec as P

D = 64
PW = 16
TILE = 128
BLK = 384
NX, NY, NZ = 4, 4, 8
PLANE = NX * NY * 2
CT = 3 * PLANE
RT = 3 * NZ
PAIRS = RT // 2
BIG = 9984.0
F32, BF16 = jnp.float32, jnp.bfloat16
MESH = pl.DeviceIdType.MESH
VMEM = pl.BlockSpec(memory_space=pltpu.VMEM)
SMEM = pl.BlockSpec(memory_space=pltpu.SMEM)


def place():
    row, col = lax.axis_index("row"), lax.axis_index("col")
    x = (col // 4) * 2 + row // 16
    return x, col % 4, (row // 2) % 8, row % 2


def device(x, y, z, core):
    return ((x % 2) * 16 + z * 2 + core, (x // 2) * 4 + y)


def slot_of(x, y, core):
    return (x % 2) * 16 + core * 8 + (x // 2) * 4 + y


def iota(shape, dim):
    return lax.broadcasted_iota(jnp.int32, shape, dim)


def norm_parts(x_t):
    floats = x_t.astype(F32)
    n = jnp.sum(floats * floats, axis=0, keepdims=True) * (-1.0 / 32.0)
    hi = n.astype(BF16).astype(F32)
    rest = n - hi
    mid = rest.astype(BF16).astype(F32)
    return hi, mid, rest - mid


def mix(rows, first, hi, mid, lo, other):
    one = jnp.where((rows >= other) & (rows < other + 3), 1.0, 0.0)
    return jnp.where(rows == first, hi, jnp.where(rows == first + 1, mid, jnp.where(rows == first + 2, lo, one)))


def lists_of(m, list_ref, info_ref):
    gram = lax.dot_general(m, m, (((1,), (1,)), ((), ())), preferred_element_type=F32)
    sub, lane = iota((RT, RT), 0), iota((RT, RT), 1)
    eye = sub == lane
    n_col = jnp.sum(m, axis=1, keepdims=True)
    n_row = jnp.sum(jnp.where(eye, gram, 0.0), axis=0, keepdims=True)
    apart = n_col + n_row - 2.0 * gram

    def key_of(overlap, apart0, ids, axis):
        score = jnp.where(apart0 > 0.5, overlap * 32.0 - ids.astype(F32), -1e6)
        return score == jnp.max(score, axis=axis, keepdims=True)

    o_row, a_row = gram[0:1, :], apart[0:1, :]
    o_col, a_col = gram[:, 0:1], apart[:, 0:1]
    e_row = key_of(o_row, a_row, lane[0:1, :], 1)
    e_col = key_of(o_col, a_col, sub[:, 0:1], 0)
    p_col = jnp.sum(jnp.where(e_row, gram, 0.0), axis=1, keepdims=True)
    p_row = jnp.sum(jnp.where(e_col, gram, 0.0), axis=0, keepdims=True)

    def order(o, p, a):
        return jnp.where(a < 0.5, 0.0, jnp.where(p > o, 1e4 - o, 2e4 + o))

    k_row, k_col = order(o_row, p_row, a_row), order(o_col, p_col, a_col)
    before = (k_col < k_row) | ((k_col == k_row) & (sub < lane))
    rank = jnp.sum(before.astype(F32), axis=0, keepdims=True)
    pair = iota((16, RT), 0).astype(F32)
    even = jnp.where(rank == 2.0 * pair, 1.0, 0.0)
    odd = jnp.where(rank == 2.0 * pair + 1.0, 1.0, 0.0)
    both = jnp.maximum(
        jnp.dot(even, m, preferred_element_type=F32), jnp.dot(odd, m, preferred_element_type=F32)
    )
    tri = jnp.where(iota((128, 128), 0) < iota((128, 128), 1), 1.0, 0.0)
    pos = jnp.dot(both, tri, preferred_element_type=F32)
    count = jnp.sum(both, axis=1, keepdims=True)
    where = jnp.where(both > 0.5, pos, -1.0)
    ids = iota((16, 128), 1)
    k = iota((128, 128), 0).astype(F32)
    prow = iota((16, 128), 0)
    total = jnp.where(ids.astype(F32) >= count, float(CT), 0.0)
    for p in range(PAIRS):
        hit = jnp.where(where[p : p + 1, :] == k, 1.0, 0.0)
        got = lax.dot_general(ids.astype(F32), hit, (((1,), (1,)), ((), ())), preferred_element_type=F32)
        total = total + jnp.where(prow == p, got, 0.0)
    list_ref[...] = total.astype(jnp.int32)
    t = iota((16, RT), 1).astype(F32)
    first = jnp.sum(even * t, axis=1, keepdims=True)
    second = jnp.sum(odd * t, axis=1, keepdims=True)
    info = jnp.where(ids == 0, first, jnp.where(ids == 1, second, jnp.where(ids == 2, count, 0.0)))
    info_ref[...] = info.astype(jnp.int32)


def gather_kernel(
    pts, pan, tp, xj, vj, xi, lists, info,
    own, colbuf, rowbuf, flags, flagbuf, mask, psend, precv, fsend, frecv, zsend, zrecv, gsend, grecv,
):
    x, y, z, core = place()
    c = (x // 2) * 4 + y
    me = slot_of(x, y, core)

    def at(d):
        return (x + d[0]) % 4, (y + d[1]) % 4

    def slot(d, which=core):
        return slot_of(*at(d), which)

    barrier = pltpu.get_barrier_semaphore()
    for o in range(1, 16):
        pl.semaphore_signal(barrier, inc=1, device_id=device(*at((o // 4, o % 4)), z, core), device_id_type=MESH)
    for o in range(1, NZ):
        pl.semaphore_signal(barrier, inc=1, device_id=device(x, y, (z + o) % NZ, core), device_id_type=MESH)
    pl.semaphore_signal(barrier, inc=1, device_id=device(x, y, z, 1 - core), device_id_type=MESH)

    own[0:D, :] = pts[...]
    own[D:, :] = pan[...]
    r, t = iota((16, 24), 0), iota((16, 24), 1)
    pick = jnp.where((r < 3) & (t == 3 * c + r), 1.0, 0.0)
    rows = jnp.dot(pick, tp[...].astype(F32), preferred_element_type=F32)
    for zz in range(NZ):
        low = rows[:, 48 * zz : 48 * zz + 48]
        high = rows[:, BLK + 48 * zz : BLK + 48 * zz + 48]
        flags[zz] = jnp.concatenate([low, high, jnp.zeros((16, 32), F32)], axis=1).astype(BF16)
    pl.semaphore_wait(barrier, 15 + NZ - 1 + 1)

    def remote(src, dst, send, recv, to):
        return pltpu.make_async_remote_copy(
            src_ref=src, dst_ref=dst, send_sem=send, recv_sem=recv, device_id=to, device_id_type=MESH
        )

    sent = []

    def start(copy):
        copy.start()
        sent.append(copy)

    def plane(src, s, d, i):
        start(remote(src, colbuf.at[s], psend.at[i], precv.at[s], device(*at(d), z, core)))

    def line(src, s, o, i):
        start(remote(src, rowbuf.at[s], zsend.at[i], zrecv.at[s], device(x, y, (z + o) % NZ, core)))

    sibling = device(x, y, z, 1 - core)

    def forward(src, s):
        start(remote(src, colbuf.at[s], fsend.at[s], frecv.at[s], sibling))

    def from_plane(s):
        remote(own, colbuf.at[s], psend.at[0], precv.at[s], sibling).wait_recv()

    def from_line(s):
        remote(own, rowbuf.at[s], zsend.at[0], zrecv.at[s], sibling).wait_recv()

    def from_sibling(s):
        remote(own, colbuf.at[s], fsend.at[s], frecv.at[s], sibling).wait_recv()

    for o in (4, 3, 5, 2, 6, 1, 7):
        to = (z + o) % NZ
        start(remote(flags.at[to], flagbuf.at[z], gsend.at[o], grecv.at[z], device(x, y, to, core)))
    near = ((1, 0), (3, 0), (0, 1), (0, 3), (1, 1), (1, 3), (3, 1), (3, 3))
    two = ((2, 0), (0, 2))
    far = ((2, 1), (2, 3), (1, 2), (3, 2), (2, 2))
    for i, o in enumerate((2, 6, 1, 7)):
        line(own, z, o, i)
    for i, d in enumerate(two + near):
        plane(own, me, d, i)
    forward(own, me)

    row64 = iota((64, TILE), 0)

    def row(zz, block):
        hi, mid, lo = norm_parts(block[0:D, :])
        for q in range(3):
            cut = slice(q * TILE, (q + 1) * TILE)
            tail = mix(row64, 0, hi[:, cut], mid[:, cut], lo[:, cut], 3)
            tail = jnp.where(row64 == 8 + 3 * zz + q, 1.0, tail)
            xi[3 * zz + q, 0:D, :] = block[0:D, cut] * jnp.bfloat16(1.0 / 16.0)
            xi[3 * zz + q, D:128, :] = tail.astype(BF16)

    lanes = iota((RT, 128), 1)

    def column(s, block):
        hi, mid, lo = norm_parts(block[0:D, :])
        for q in range(3):
            cut = slice(q * TILE, (q + 1) * TILE)
            tail = mix(row64[0:8], 3, hi[:, cut], mid[:, cut], lo[:, cut], 0)
            on = jnp.sum(jnp.where(lanes == 3 * s + q, mask[...], 0.0), axis=1, keepdims=True)
            off = jnp.broadcast_to((on - 1.0) * BIG, (RT, TILE))
            feats = jnp.concatenate(
                [block[0:D, cut].astype(F32), tail, off, jnp.zeros((128 - D - 8 - RT, TILE), F32)], axis=0
            )
            xj[3 * s + q] = feats.T.astype(BF16)
            vj[3 * s + q] = block[D:, cut]

    xj[CT] = jnp.zeros((TILE, TILE), BF16)
    vj[CT] = jnp.zeros((PW, TILE), BF16)
    row(z, own[...])

    s = slot((2, 0))
    from_plane(s)
    plane(colbuf.at[s], s, (0, 1), 10)
    plane(colbuf.at[s], s, (0, 3), 11)
    s = slot((0, 2))
    from_plane(s)
    plane(colbuf.at[s], s, (1, 0), 12)
    plane(colbuf.at[s], s, (3, 0), 13)
    s = slot((2 * (1 - core), 2 * core))
    plane(colbuf.at[s], s, (2 * core, 2 * (1 - core)), 14)
    s = (z + 6) % NZ
    from_line(s)
    line(rowbuf.at[s], s, 1, 4)
    line(rowbuf.at[s], s, 2, 5)
    s = (z + 2) % NZ
    from_line(s)
    line(rowbuf.at[s], s, 7, 6)
    for d in two:
        forward(colbuf.at[slot(d)], slot(d))

    for o in range(1, NZ):
        zz = (z + o) % NZ
        remote(flags.at[0], flagbuf.at[zz], gsend.at[o], grecv.at[zz], sibling).wait_recv()
    flagbuf[z] = flags[z]
    for zz in range(NZ):
        mask[3 * zz : 3 * zz + 3, :] = flagbuf[zz].astype(F32)[0:3, :]
    lists_of(mask[...], lists, info)
    column(me, own[...])
    for d in two:
        column(slot(d), colbuf[slot(d)])
    for d in near:
        from_plane(slot(d))
        forward(colbuf.at[slot(d)], slot(d))
        column(slot(d), colbuf[slot(d)])
    for o in (2, 6, 1, 7):
        zz = (z + o) % NZ
        if o in (1, 7):
            from_line(zz)
        row(zz, rowbuf[zz])
    first = ((0, 0),) + two + near
    for d in first[:3]:
        s = slot(d, 1 - core)
        from_sibling(s)
        column(s, colbuf[s])
    for d in far:
        from_plane(slot(d))
        forward(colbuf.at[slot(d)], slot(d))
    for d in far:
        column(slot(d), colbuf[slot(d)])
    for d in first[3:]:
        s = slot(d, 1 - core)
        from_sibling(s)
        column(s, colbuf[s])
    for o in (3, 5, 4):
        zz = (z + o) % NZ
        from_line(zz)
        row(zz, rowbuf[zz])
    for d in far:
        s = slot(d, 1 - core)
        from_sibling(s)
        column(s, colbuf[s])
    for copy in sent:
        copy.wait_send()


JT = 8
SUB = 8


def apply_kernel(lists, info, xj, vj, xi, out, *held):
    out[...] = jnp.zeros_like(out)

    def weights(p):
        return jnp.concatenate([xi[info[p, 0]], xi[info[p, 1]]], axis=1)

    def compute(p, k, q, w, held_ref):
        s = jnp.dot(xj[lists[p, k + q]], w, preferred_element_type=F32)
        held_ref[q * TILE : (q + 1) * TILE, :] = jnp.exp(jnp.minimum(s, 0.0)).astype(BF16)

    def apply(p, k, q, held_ref):
        v = jnp.concatenate([vj[lists[p, k + q]], vj[lists[p, k + q + 1]]], axis=1)
        return jnp.dot(v, held_ref[q * TILE : (q + 2) * TILE, :], preferred_element_type=F32)

    def following(p, k):
        end = k + JT >= info[p, 2]
        last = p == PAIRS - 1
        k = jnp.where(end, jnp.where(last, 100, 0), k + JT)
        return jnp.where(end & ~last, p + 1, p), k

    total = sum(jnp.maximum((info[p, 2] + JT - 1) // JT, 1) for p in range(PAIRS))
    zero = jnp.int32(0)
    w = weights(zero)
    for q in range(JT):
        compute(zero, zero, q, w, held[SUB - 1])

    def step(_, at):
        for u in range(SUB):
            nxt = following(*at)
            w = weights(nxt[0])
            r = None
            for q in range(JT):
                compute(*nxt, q, w, held[u])
                if q % 2 == 0:
                    part = apply(*at, q, held[u - 1])
                    r = part if r is None else r + part
            a, b = info[at[0], 0], info[at[0], 1]
            out[a] += r[:, :TILE]
            out[b] += r[:, TILE:]
            at = nxt
        return at

    lax.fori_loop(0, (total + SUB - 1) // SUB, step, (zero, zero))


def reduce_kernel(part, out, got, send, recv):
    x, y, z, core = place()
    barrier = pltpu.get_barrier_semaphore()
    for o in range(1, NZ):
        pl.semaphore_signal(barrier, inc=1, device_id=device(x, y, (z + o) % NZ, core), device_id_type=MESH)
    pl.semaphore_wait(barrier, NZ - 1)

    def copy(o, slot):
        to = (z + o) % NZ
        return pltpu.make_async_remote_copy(
            src_ref=part.at[pl.ds(3 * to, 3)],
            dst_ref=got.at[slot],
            send_sem=send.at[o],
            recv_sem=recv.at[slot],
            device_id=device(x, y, to, core),
            device_id_type=MESH,
        )

    for o in (4, 3, 5, 2, 6, 1, 7):
        copy(o, z).start()
    total = [part[3 * z + q] for q in range(3)]
    for o in (1, 7, 2, 6, 3, 5, 4):
        zz = (z + o) % NZ
        copy(o, zz).wait_recv()
        total = [total[q] + got[zz, q] for q in range(3)]
    for q in range(3):
        out[:, q * TILE : (q + 1) * TILE] = total[q]
    for o in range(1, NZ):
        copy(o, z).wait_send()


def local(points, panel, tile_pairs):
    shape = jax.ShapeDtypeStruct
    dma = pltpu.SemaphoreType.DMA
    xj, vj, xi, lists, info = pl.pallas_call(
        gather_kernel,
        out_shape=(
            shape((CT + 1, TILE, TILE), BF16),
            shape((CT + 1, PW, TILE), BF16),
            shape((RT, TILE, TILE), BF16),
            shape((16, 128), jnp.int32),
            shape((16, 128), jnp.int32),
        ),
        in_specs=[VMEM] * 3,
        out_specs=[VMEM] * 5,
        scratch_shapes=[
            pltpu.VMEM((D + PW, BLK), BF16),
            pltpu.VMEM((PLANE, D + PW, BLK), BF16),
            pltpu.VMEM((NZ, D + PW, BLK), BF16),
            pltpu.VMEM((NZ, 16, 128), BF16),
            pltpu.VMEM((NZ, 16, 128), BF16),
            pltpu.VMEM((RT, 128), F32),
            dma((16,)),
            dma((PLANE,)),
            dma((PLANE,)),
            dma((PLANE,)),
            dma((NZ,)),
            dma((NZ,)),
            dma((NZ,)),
            dma((NZ,)),
        ],
        compiler_params=pltpu.CompilerParams(
            collective_id=0, has_side_effects=True, vmem_limit_bytes=40 * 2**20
        ),
        name="gather",
    )(points.T, panel.T, tile_pairs)
    part = pl.pallas_call(
        apply_kernel,
        out_shape=shape((RT, PW, TILE), F32),
        in_specs=[SMEM, SMEM, VMEM, VMEM, VMEM],
        out_specs=VMEM,
        scratch_shapes=[pltpu.VMEM((JT * TILE, 2 * TILE), BF16)] * SUB,
        compiler_params=pltpu.CompilerParams(vmem_limit_bytes=40 * 2**20),
        name="apply",
    )(lists, info, xj, vj, xi)
    return pl.pallas_call(
        reduce_kernel,
        out_shape=shape((PW, BLK), F32),
        in_specs=[VMEM],
        out_specs=VMEM,
        scratch_shapes=[pltpu.VMEM((NZ, 3, PW, TILE), F32), dma((NZ,)), dma((NZ,))],
        compiler_params=pltpu.CompilerParams(
            collective_id=1, has_side_effects=True, vmem_limit_bytes=40 * 2**20
        ),
        name="reduce",
    )(part).T


def solution(mesh):
    in_specs = (P(("row", "col"), None), P(("row", "col"), None), P("row", None))
    out_specs = P(("row", "col"), None)
    return jax.shard_map(local, mesh=mesh, in_specs=in_specs, out_specs=out_specs, check_vma=False)
```

time: 75.1 us -> 54.9 us (0.73)
  Pallas kernels: 71.5 us -> 51.7 us
    pallas_call x1, Pallas kernels: 28.6 us -> 18.1 us  [local(): pl.pallas_call(apply_kernel, out_shape=shape((RT, PW, TILE), F32), in_spe...]
    pallas_call x1, Pallas kernels: 32.8 us -> 23.2 us  [local(): pl.pallas_call(gather_kernel, out_shape=(shape((CT + 1, TILE, TILE), BF16...]
    unnamed x4 -> x7, local copies, waits for them, and re-layouts: 2.62 us -> 3 us
where the time goes in v2:
time: 54.9 us; the launch traced here: 54.7 us
  Pallas kernels  51.7 us (94%)
  local copies, waits for them, and re-layouts  3 us (5%)
    pallas_call x1, Pallas kernels, local(): pl.pallas_call(gather_kernel, out_shape=(shape((CT + 1, TILE, TILE), BF16...  23.2 us
    pallas_call x1, Pallas kernels, local(): pl.pallas_call(apply_kernel, out_shape=shape((RT, PW, TILE), F32), in_spe...  18.1 us
    pallas_call x1, Pallas kernels, local(): pl.pallas_call(reduce_kernel, out_shape=shape((PW, BLK), F32), in_specs=[...  10.3 us
    unnamed x7, local copies, waits for them, and re-layouts  3 us

profile of v2, /device:TPU:8, one launch (start us, length us, event | category | flops | bytes accessed | tf_op | source)
XLA Modules:
  0.0 54.7 jit_solution(7831009497318302632)
XLA Ops:
  0.0 0.0 copy-start
  0.0 0.9 %copy-done = s32[24,768]{1,0:T(8,128)S(1)} copy-done((s32[24,768]{1,0:T(8,128)S(1)}, s32[24,768]{1,0:T(8,128)}, u32[]{:S(2)}) %copy-start) | copy-done | bytes 73752
  0.9 0.0 copy-start.1
  0.9 0.8 %copy-done.1 = bf16[384,64]{0,1:T(8,128)(2,1)S(1)} copy-done((bf16[384,64]{0,1:T(8,128)(2,1)S(1)}, bf16[384,64]{0,1:T(8,128)(2,1)}, u32[]{:S(2)}) %copy-start.1) | copy-done | bytes 49176
  1.7 0.0 copy-start.2
  1.7 0.7 %copy-done.2 = bf16[384,16]{0,1:T(8,128)(2,1)S(1)} copy-done((bf16[384,16]{0,1:T(8,128)(2,1)S(1)}, bf16[384,16]{0,1:T(8,128)(2,1)}, u32[]{:S(2)}) %copy-start.2) | copy-done | bytes 12312
  2.4 23.2 %gather.1 = (bf16[97,128,128]{2,1,0:T(8,128)(2,1)S(1)}, bf16[97,16,128]{2,1,0:T(8,128)(2,1)S(1)}, bf16[24,128,128]{2,1,0:T(8,128)(2,1)S(1)}, s32[16,128]{1,0:T(8,128)S(1)}, s32[16,128]{1,0:T(8,128)S(1)}) custom-call(bf16[64,384]{1,0:T(8,128)(2,1)S(1)} %bitcast.4, bf16[16,384]{1,0:T(8,128)(2,1)S(1)} %bitcast.5, s32[24,768]{1,0:T(8,128)S(1)} %copy-done), custom_call_target="tpu_custom_call" | custom-call | tf_op jit(solution)/shard_map/gather/pallas_call | solution.py:360
  25.6 18.1 %apply.1.part = f32[24,16,128]{2,1,0:T(8,128)S(1)} custom-call(s32[16,128]{1,0:T(8,128)S(1)} %get-tuple-element.10.lists, s32[16,128]{1,0:T(8,128)S(1)} %get-tuple-element.11.info, bf16[97,128,128]{2,1,0:T(8,128)(2,1)S(1)} %get-tuple-element.12.xj, bf16[97,16,128]{2,1,0:T(8,128)(2,1)S(1)} %get-tuple-element.13.vj, bf16[24,128,128]{2,1,0:T(8,128)(2,1)S(1)} %get-tuple-element.14.xi), custom_call_target="tpu_custom_call" | custom-call | tf_op jit(solution)/shard_map/apply/pallas_call | solution.py:392
  43.8 10.3 %reduce.1 = f32[16,384]{1,0:T(8,128)S(1)} custom-call(f32[24,16,128]{2,1,0:T(8,128)S(1)} %apply.1.part), custom_call_target="tpu_custom_call" | custom-call | tf_op jit(solution)/shard_map/reduce/pallas_call | solution.py:401
  54.1 0.6 %copy.5 = f32[384,16]{0,1:T(8,128)} copy(f32[384,16]{0,1:T(8,128)S(1)} %bitcast.3) | data formatting | bytes 49152
Async XLA Ops:
  0.0 0.9 %copy-start = (s32[24,768]{1,0:T(8,128)S(1)}, s32[24,768]{1,0:T(8,128)}, u32[]{:S(2)}) copy-start(s32[24,768]{1,0:T(8,128)} %tp.1) | copy-start | bytes 221188
  0.9 0.8 %copy-start.1 = (bf16[384,64]{0,1:T(8,128)(2,1)S(1)}, bf16[384,64]{0,1:T(8,128)(2,1)}, u32[]{:S(2)}) copy-start(bf16[384,64]{0,1:T(8,128)(2,1)} %param.3) | copy-start | bytes 147460
  1.7 0.7 %copy-start.2 = (bf16[384,16]{0,1:T(8,128)(2,1)S(1)}, bf16[384,16]{0,1:T(8,128)(2,1)}, u32[]{:S(2)}) copy-start(bf16[384,16]{0,1:T(8,128)(2,1)} %param.4) | copy-start | bytes 36868

commit v3 on v2

--- a/solution.py
+++ b/solution.py
@@ -13,11 +13,12 @@
 PLANE = NX * NY * 2
 CT = 3 * PLANE
 RT = 3 * NZ
-PAIRS = RT // 2
+PAIRS = (RT - 2) // 2
 BIG = 9984.0
 F32, BF16 = jnp.float32, jnp.bfloat16
 MESH = pl.DeviceIdType.MESH
 VMEM = pl.BlockSpec(memory_space=pltpu.VMEM)
+HBM = pl.BlockSpec(memory_space=pltpu.HBM)
 SMEM = pl.BlockSpec(memory_space=pltpu.SMEM)
 
 
@@ -53,7 +54,7 @@
     return jnp.where(rows == first, hi, jnp.where(rows == first + 1, mid, jnp.where(rows == first + 2, lo, one)))
 
 
-def lists_of(m, list_ref, info_ref):
+def lists_of(m, z, list_ref, info_ref):
     gram = lax.dot_general(m, m, (((1,), (1,)), ((), ())), preferred_element_type=F32)
     sub, lane = iota((RT, RT), 0), iota((RT, RT), 1)
     eye = sub == lane
@@ -75,12 +76,17 @@
     def order(o, p, a):
         return jnp.where(a < 0.5, 0.0, jnp.where(p > o, 1e4 - o, 2e4 + o))
 
-    k_row, k_col = order(o_row, p_row, a_row), order(o_col, p_col, a_col)
+    def mine(ids):
+        return (ids >= 3 * z) & (ids < 3 * z + 3)
+
+    k_row = jnp.where(mine(lane[0:1, :]), 1e6, order(o_row, p_row, a_row))
+    k_col = jnp.where(mine(sub[:, 0:1]), 1e6, order(o_col, p_col, a_col))
     before = (k_col < k_row) | ((k_col == k_row) & (sub < lane))
     rank = jnp.sum(before.astype(F32), axis=0, keepdims=True)
     pair = iota((16, RT), 0).astype(F32)
     even = jnp.where(rank == 2.0 * pair, 1.0, 0.0)
     odd = jnp.where(rank == 2.0 * pair + 1.0, 1.0, 0.0)
+    m = jnp.where(mine(iota((RT, 128), 0)), 0.0, m)
     both = jnp.maximum(
         jnp.dot(even, m, preferred_element_type=F32), jnp.dot(odd, m, preferred_element_type=F32)
     )
@@ -106,7 +112,7 @@
 
 def gather_kernel(
     pts, pan, tp, xj, vj, xi, lists, info,
-    own, colbuf, rowbuf, flags, flagbuf, mask, psend, precv, fsend, frecv, zsend, zrecv, gsend, grecv,
+    own, pairs, colbuf, rowbuf, flags, flagbuf, mask, local, psend, precv, fsend, frecv, zsend, zrecv, gsend, grecv,
 ):
     x, y, z, core = place()
     c = (x // 2) * 4 + y
@@ -118,6 +124,13 @@
     def slot(d, which=core):
         return slot_of(*at(d), which)
 
+    fetch = [
+        pltpu.make_async_copy(pts, own.at[0:D], local.at[0]),
+        pltpu.make_async_copy(pan, own.at[D : D + PW], local.at[1]),
+        pltpu.make_async_copy(tp, pairs, local.at[2]),
+    ]
+    for copy in fetch:
+        copy.start()
     barrier = pltpu.get_barrier_semaphore()
     for o in range(1, 16):
         pl.semaphore_signal(barrier, inc=1, device_id=device(*at((o // 4, o % 4)), z, core), device_id_type=MESH)
@@ -125,11 +138,11 @@
         pl.semaphore_signal(barrier, inc=1, device_id=device(x, y, (z + o) % NZ, core), device_id_type=MESH)
     pl.semaphore_signal(barrier, inc=1, device_id=device(x, y, z, 1 - core), device_id_type=MESH)
 
-    own[0:D, :] = pts[...]
-    own[D:, :] = pan[...]
+    for copy in fetch:
+        copy.wait()
     r, t = iota((16, 24), 0), iota((16, 24), 1)
     pick = jnp.where((r < 3) & (t == 3 * c + r), 1.0, 0.0)
-    rows = jnp.dot(pick, tp[...].astype(F32), preferred_element_type=F32)
+    rows = jnp.dot(pick, pairs[...].astype(F32), preferred_element_type=F32)
     for zz in range(NZ):
         low = rows[:, 48 * zz : 48 * zz + 48]
         high = rows[:, BLK + 48 * zz : BLK + 48 * zz + 48]
@@ -235,7 +248,7 @@
     flagbuf[z] = flags[z]
     for zz in range(NZ):
         mask[3 * zz : 3 * zz + 3, :] = flagbuf[zz].astype(F32)[0:3, :]
-    lists_of(mask[...], lists, info)
+    lists_of(mask[...], z, lists, info)
     column(me, own[...])
     for d in two:
         column(slot(d), colbuf[slot(d)])
@@ -323,7 +336,7 @@
     lax.fori_loop(0, (total + SUB - 1) // SUB, step, (zero, zero))
 
 
-def reduce_kernel(part, out, got, send, recv):
+def reduce_kernel(part, xj, vj, xi, out, got, held, total, send, recv):
     x, y, z, core = place()
     barrier = pltpu.get_barrier_semaphore()
     for o in range(1, NZ):
@@ -343,13 +356,37 @@
 
     for o in (4, 3, 5, 2, 6, 1, 7):
         copy(o, z).start()
-    total = [part[3 * z + q] for q in range(3)]
+
+    w = jnp.concatenate([xi[3 * z + q] for q in range(3)], axis=1)
+    some = 8
+
+    def compute(j, q, slot):
+        s = jnp.dot(xj[j * some + q], w, preferred_element_type=F32)
+        held[slot, q * TILE : (q + 1) * TILE, :] = jnp.exp(jnp.minimum(s, 0.0)).astype(BF16)
+
+    def apply(j, q, slot):
+        v = jnp.concatenate([vj[j * some + q], vj[j * some + q + 1]], axis=1)
+        return jnp.dot(v, held[slot, q * TILE : (q + 2) * TILE, :], preferred_element_type=F32)
+
+    for q in range(some):
+        compute(0, q, 1)
+
+    def step(t, acc):
+        for u in range(4):
+            j = 4 * t + u
+            for q in range(some):
+                compute(jnp.minimum(j + 1, CT // some - 1), q, u % 2)
+                if q % 2 == 0:
+                    acc = acc + apply(j, q, 1 - u % 2)
+        return acc
+
+    total[...] = lax.fori_loop(0, CT // some // 4, step, jnp.zeros((PW, BLK), F32))
     for o in (1, 7, 2, 6, 3, 5, 4):
         zz = (z + o) % NZ
         copy(o, zz).wait_recv()
-        total = [total[q] + got[zz, q] for q in range(3)]
-    for q in range(3):
-        out[:, q * TILE : (q + 1) * TILE] = total[q]
+        for q in range(3):
+            total[:, q * TILE : (q + 1) * TILE] += got[zz, q]
+    out[...] = total[...]
     for o in range(1, NZ):
         copy(o, z).wait_send()
 
@@ -366,15 +403,17 @@
             shape((16, 128), jnp.int32),
             shape((16, 128), jnp.int32),
         ),
-        in_specs=[VMEM] * 3,
+        in_specs=[HBM] * 3,
         out_specs=[VMEM] * 5,
         scratch_shapes=[
             pltpu.VMEM((D + PW, BLK), BF16),
+            pltpu.VMEM((RT, CT * NZ), jnp.int32),
             pltpu.VMEM((PLANE, D + PW, BLK), BF16),
             pltpu.VMEM((NZ, D + PW, BLK), BF16),
             pltpu.VMEM((NZ, 16, 128), BF16),
             pltpu.VMEM((NZ, 16, 128), BF16),
             pltpu.VMEM((RT, 128), F32),
+            dma((3,)),
             dma((16,)),
             dma((PLANE,)),
             dma((PLANE,)),
@@ -388,7 +427,7 @@
             collective_id=0, has_side_effects=True, vmem_limit_bytes=40 * 2**20
         ),
         name="gather",
-    )(points.T, panel.T, tile_pairs)
+    )(*(pltpu.with_memory_space_constraint(a, pltpu.HBM) for a in (points.T, panel.T, tile_pairs)))
     part = pl.pallas_call(
         apply_kernel,
         out_shape=shape((RT, PW, TILE), F32),
@@ -401,14 +440,20 @@
     return pl.pallas_call(
         reduce_kernel,
         out_shape=shape((PW, BLK), F32),
-        in_specs=[VMEM],
+        in_specs=[VMEM] * 4,
         out_specs=VMEM,
-        scratch_shapes=[pltpu.VMEM((NZ, 3, PW, TILE), F32), dma((NZ,)), dma((NZ,))],
+        scratch_shapes=[
+            pltpu.VMEM((NZ, 3, PW, TILE), F32),
+            pltpu.VMEM((2, 8 * TILE, BLK), BF16),
+            pltpu.VMEM((PW, BLK), F32),
+            dma((NZ,)),
+            dma((NZ,)),
+        ],
         compiler_params=pltpu.CompilerParams(
             collective_id=1, has_side_effects=True, vmem_limit_bytes=40 * 2**20
         ),
         name="reduce",
-    )(part).T
+    )(part, xj, vj, xi).T
 
 
 def solution(mesh):

time: 54.9 us -> 53.8 us (0.980)
  the two profiles are of different devices: /device:TPU:8 before, /device:TPU:1 now
where the time goes in v3:
time: 53.8 us; the launch traced here: 53.7 us
  Pallas kernels  53 us (99%)
  local copies, waits for them, and re-layouts  0.61 us (1%)
    pallas_call x1, Pallas kernels, local(): pl.pallas_call(gather_kernel, out_shape=(shape((CT + 1, TILE, TILE), BF16...  23.8 us
    pallas_call x1, Pallas kernels, local(): pl.pallas_call(apply_kernel, out_shape=shape((RT, PW, TILE), F32), in_spe...  18 us
    pallas_call x1, Pallas kernels, local(): pl.pallas_call(reduce_kernel, out_shape=shape((PW, BLK), F32), in_specs=[...  11.2 us

profile of v3, /device:TPU:1, one launch (start us, length us, event | category | flops | bytes accessed | tf_op | source)
XLA Modules:
  0.0 53.7 jit_solution(15922177537680906532)
XLA Ops:
  0.0 23.8 %gather.1 = (bf16[97,128,128]{2,1,0:T(8,128)(2,1)S(1)}, bf16[97,16,128]{2,1,0:T(8,128)(2,1)S(1)}, bf16[24,128,128]{2,1,0:T(8,128)(2,1)S(1)}, s32[16,128]{1,0:T(8,128)S(1)}, s32[16,128]{1,0:T(8,128)S(1)}) custom-call(bf16[64,384]{1,0:T(8,128)(2,1)} %bitcast.4, bf16[16,384]{1,0:T(8,128)(2,1)} %bitcast.5, s32[24,768]{1,0:T(8,128)} %tp.1), custom_call_target="tpu_custom_call" | custom-call | tf_op jit(solution)/shard_map/gather/pallas_call | solution.py:397
  23.8 18.0 %apply.1.part = f32[24,16,128]{2,1,0:T(8,128)S(1)} custom-call(s32[16,128]{1,0:T(8,128)S(1)} %get-tuple-element.10.lists, s32[16,128]{1,0:T(8,128)S(1)} %get-tuple-element.11.info, bf16[97,128,128]{2,1,0:T(8,128)(2,1)S(1)} %get-tuple-element.12.xj, bf16[97,16,128]{2,1,0:T(8,128)(2,1)S(1)} %get-tuple-element.13.vj, bf16[24,128,128]{2,1,0:T(8,128)(2,1)S(1)} %get-tuple-element.14.xi), custom_call_target="tpu_custom_call" | custom-call | tf_op jit(solution)/shard_map/apply/pallas_call | solution.py:431
  41.8 11.2 %reduce.1 = f32[16,384]{1,0:T(8,128)S(1)} custom-call(f32[24,16,128]{2,1,0:T(8,128)S(1)} %apply.1.part, bf16[97,128,128]{2,1,0:T(8,128)(2,1)S(1)} %get-tuple-element.12.xj, bf16[97,16,128]{2,1,0:T(8,128)(2,1)S(1)} %get-tuple-element.13.vj, bf16[24,128,128]{2,1,0:T(8,128)(2,1)S(1)} %get-tuple-element.14.xi), custom_call_target="tpu_custom_call" | custom-call | tf_op jit(solution)/shard_map/reduce/pallas_call | solution.py:440
  53.0 0.6 %copy.5 = f32[384,16]{0,1:T(8,128)} copy(f32[384,16]{0,1:T(8,128)S(1)} %bitcast.3) | data formatting | bytes 49152

commit v4 on v3

--- a/solution.py
+++ b/solution.py
@@ -112,7 +112,7 @@
 
 def gather_kernel(
     pts, pan, tp, xj, vj, xi, lists, info,
-    own, pairs, colbuf, rowbuf, flags, flagbuf, mask, local, psend, precv, fsend, frecv, zsend, zrecv, gsend, grecv,
+    own, pairs, colbuf, rowbuf, flags, flagbuf, up, down, mask, local, psend, precv, fsend, frecv, zsend, zrecv, gsend, grecv,
 ):
     x, y, z, core = place()
     c = (x // 2) * 4 + y
@@ -132,9 +132,12 @@
     for copy in fetch:
         copy.start()
     barrier = pltpu.get_barrier_semaphore()
-    for o in range(1, 16):
-        pl.semaphore_signal(barrier, inc=1, device_id=device(*at((o // 4, o % 4)), z, core), device_id_type=MESH)
-    for o in range(1, NZ):
+    near = ((1, 0), (3, 0), (0, 1), (0, 3), (1, 1), (1, 3), (3, 1), (3, 3))
+    two = ((2, 0), (0, 2))
+    far = ((2, 1), (2, 3), (1, 2), (3, 2), (2, 2))
+    for d in two + near:
+        pl.semaphore_signal(barrier, inc=1, device_id=device(*at(d), z, core), device_id_type=MESH)
+    for o in (1, 2, 6, 7):
         pl.semaphore_signal(barrier, inc=1, device_id=device(x, y, (z + o) % NZ, core), device_id_type=MESH)
     pl.semaphore_signal(barrier, inc=1, device_id=device(x, y, z, 1 - core), device_id_type=MESH)
 
@@ -146,8 +149,8 @@
     for zz in range(NZ):
         low = rows[:, 48 * zz : 48 * zz + 48]
         high = rows[:, BLK + 48 * zz : BLK + 48 * zz + 48]
-        flags[zz] = jnp.concatenate([low, high, jnp.zeros((16, 32), F32)], axis=1).astype(BF16)
-    pl.semaphore_wait(barrier, 15 + NZ - 1 + 1)
+        flags[(zz - z + NZ) % NZ] = jnp.concatenate([low, high, jnp.zeros((16, 32), F32)], axis=1).astype(BF16)
+    pl.semaphore_wait(barrier, 10 + 4 + 1)
 
     def remote(src, dst, send, recv, to):
         return pltpu.make_async_remote_copy(
@@ -175,19 +178,23 @@
         remote(own, colbuf.at[s], psend.at[0], precv.at[s], sibling).wait_recv()
 
     def from_line(s):
-        remote(own, rowbuf.at[s], zsend.at[0], zrecv.at[s], sibling).wait_recv()
+        remote(own.at[0:D], rowbuf.at[s], zsend.at[0], zrecv.at[s], sibling).wait_recv()
 
     def from_sibling(s):
         remote(own, colbuf.at[s], fsend.at[s], frecv.at[s], sibling).wait_recv()
 
-    for o in (4, 3, 5, 2, 6, 1, 7):
-        to = (z + o) % NZ
-        start(remote(flags.at[to], flagbuf.at[z], gsend.at[o], grecv.at[z], device(x, y, to, core)))
-    near = ((1, 0), (3, 0), (0, 1), (0, 3), (1, 1), (1, 3), (3, 1), (3, 3))
-    two = ((2, 0), (0, 2))
-    far = ((2, 1), (2, 3), (1, 2), (3, 2), (2, 2))
+    def flag(src, dst, o, i, s):
+        start(remote(src, dst, gsend.at[i], grecv.at[s], device(x, y, (z + o) % NZ, core)))
+
+    def from_flag(dst, s):
+        remote(dst, dst, gsend.at[0], grecv.at[s], sibling).wait_recv()
+
+    flag(flags.at[2:5], up, 2, 0, NZ)
+    flag(flags.at[5:7], down, 6, 1, NZ + 1)
+    flag(flags.at[1], flagbuf.at[z], 1, 2, z)
+    flag(flags.at[7], flagbuf.at[z], 7, 3, z)
     for i, o in enumerate((2, 6, 1, 7)):
-        line(own, z, o, i)
+        line(own.at[0:D], z, o, i)
     for i, d in enumerate(two + near):
         plane(own, me, d, i)
     forward(own, me)
@@ -221,6 +228,12 @@
     xj[CT] = jnp.zeros((TILE, TILE), BF16)
     vj[CT] = jnp.zeros((PW, TILE), BF16)
     row(z, own[...])
+    below, above = (z + 6) % NZ, (z + 2) % NZ
+    from_flag(up, NZ)
+    flag(up.at[1], flagbuf.at[below], 1, 4, below)
+    flag(up.at[2], flagbuf.at[below], 2, 5, below)
+    from_flag(down, NZ + 1)
+    flag(down.at[0], flagbuf.at[above], 7, 6, above)
 
     s = slot((2, 0))
     from_plane(s)
@@ -232,63 +245,67 @@
     plane(colbuf.at[s], s, (3, 0), 13)
     s = slot((2 * (1 - core), 2 * core))
     plane(colbuf.at[s], s, (2 * core, 2 * (1 - core)), 14)
-    s = (z + 6) % NZ
-    from_line(s)
-    line(rowbuf.at[s], s, 1, 4)
-    line(rowbuf.at[s], s, 2, 5)
-    s = (z + 2) % NZ
-    from_line(s)
-    line(rowbuf.at[s], s, 7, 6)
+    from_line(below)
+    line(rowbuf.at[below], below, 1, 4)
+    line(rowbuf.at[below], below, 2, 5)
+    from_line(above)
+    line(rowbuf.at[above], above, 7, 6)
     for d in two:
         forward(colbuf.at[slot(d)], slot(d))
-
-    for o in range(1, NZ):
+    side, diagonal = near[:4], near[4:]
+    for d in side:
+        from_plane(slot(d))
+        forward(colbuf.at[slot(d)], slot(d))
+    row(below, rowbuf[below])
+    row(above, rowbuf[above])
+    for o in (1, 7):
         zz = (z + o) % NZ
-        remote(flags.at[0], flagbuf.at[zz], gsend.at[o], grecv.at[zz], sibling).wait_recv()
-    flagbuf[z] = flags[z]
+        from_line(zz)
+        row(zz, rowbuf[zz])
+
+    for d in diagonal:
+        from_plane(slot(d))
+        forward(colbuf.at[slot(d)], slot(d))
+
+    for o in (1, 7, 3, 4, 5):
+        from_flag(flagbuf.at[(z + o) % NZ], (z + o) % NZ)
+    flagbuf[z] = flags[0]
+    flagbuf[below] = up[0]
+    flagbuf[above] = down[1]
     for zz in range(NZ):
         mask[3 * zz : 3 * zz + 3, :] = flagbuf[zz].astype(F32)[0:3, :]
-    lists_of(mask[...], z, lists, info)
     column(me, own[...])
-    for d in two:
+    for d in two + side + diagonal:
         column(slot(d), colbuf[slot(d)])
-    for d in near:
-        from_plane(slot(d))
-        forward(colbuf.at[slot(d)], slot(d))
-        column(slot(d), colbuf[slot(d)])
-    for o in (2, 6, 1, 7):
-        zz = (z + o) % NZ
-        if o in (1, 7):
-            from_line(zz)
-        row(zz, rowbuf[zz])
-    first = ((0, 0),) + two + near
-    for d in first[:3]:
+
+    def other(d):
         s = slot(d, 1 - core)
         from_sibling(s)
         column(s, colbuf[s])
+
+    lists_of(mask[...], z, lists, info)
     for d in far:
         from_plane(slot(d))
         forward(colbuf.at[slot(d)], slot(d))
-    for d in far:
-        column(slot(d), colbuf[slot(d)])
-    for d in first[3:]:
-        s = slot(d, 1 - core)
-        from_sibling(s)
-        column(s, colbuf[s])
+    for d in ((0, 0),) + two + side:
+        other(d)
+    for d in diagonal:
+        other(d)
     for o in (3, 5, 4):
         zz = (z + o) % NZ
         from_line(zz)
         row(zz, rowbuf[zz])
     for d in far:
-        s = slot(d, 1 - core)
-        from_sibling(s)
-        column(s, colbuf[s])
+        column(slot(d), colbuf[slot(d)])
+    for d in far:
+        other(d)
     for copy in sent:
         copy.wait_send()
 
 
 JT = 8
-SUB = 8
+STEPS = (16, 4)
+HELD = 4
 
 
 def apply_kernel(lists, info, xj, vj, xi, out, *held):
@@ -315,25 +332,31 @@
     zero = jnp.int32(0)
     w = weights(zero)
     for q in range(JT):
-        compute(zero, zero, q, w, held[SUB - 1])
-
-    def step(_, at):
-        for u in range(SUB):
-            nxt = following(*at)
-            w = weights(nxt[0])
-            r = None
-            for q in range(JT):
-                compute(*nxt, q, w, held[u])
-                if q % 2 == 0:
-                    part = apply(*at, q, held[u - 1])
-                    r = part if r is None else r + part
-            a, b = info[at[0], 0], info[at[0], 1]
-            out[a] += r[:, :TILE]
-            out[b] += r[:, TILE:]
-            at = nxt
-        return at
-
-    lax.fori_loop(0, (total + SUB - 1) // SUB, step, (zero, zero))
+        compute(zero, zero, q, w, held[HELD - 1])
+
+    def steps(some):
+        def step(_, at):
+            for u in range(some):
+                nxt = following(*at)
+                w = weights(nxt[0])
+                r = None
+                for q in range(JT):
+                    compute(*nxt, q, w, held[u % HELD])
+                    if q % 2 == 0:
+                        part = apply(*at, q, held[(u - 1) % HELD])
+                        r = part if r is None else r + part
+                a, b = info[at[0], 0], info[at[0], 1]
+                out[a] += r[:, :TILE]
+                out[b] += r[:, TILE:]
+                at = nxt
+            return at
+
+        return step
+
+    many, few = STEPS
+    whole = total // many
+    at = lax.fori_loop(0, whole, steps(many), (zero, zero))
+    lax.fori_loop(0, (total - whole * many + few - 1) // few, steps(few), at)
 
 
 def reduce_kernel(part, xj, vj, xi, out, got, held, total, send, recv):
@@ -409,9 +432,11 @@
             pltpu.VMEM((D + PW, BLK), BF16),
             pltpu.VMEM((RT, CT * NZ), jnp.int32),
             pltpu.VMEM((PLANE, D + PW, BLK), BF16),
-            pltpu.VMEM((NZ, D + PW, BLK), BF16),
+            pltpu.VMEM((NZ, D, BLK), BF16),
             pltpu.VMEM((NZ, 16, 128), BF16),
             pltpu.VMEM((NZ, 16, 128), BF16),
+            pltpu.VMEM((3, 16, 128), BF16),
+            pltpu.VMEM((2, 16, 128), BF16),
             pltpu.VMEM((RT, 128), F32),
             dma((3,)),
             dma((16,)),
@@ -421,7 +446,7 @@
             dma((NZ,)),
             dma((NZ,)),
             dma((NZ,)),
-            dma((NZ,)),
+            dma((NZ + 2,)),
         ],
         compiler_params=pltpu.CompilerParams(
             collective_id=0, has_side_effects=True, vmem_limit_bytes=40 * 2**20
@@ -433,7 +458,7 @@
         out_shape=shape((RT, PW, TILE), F32),
         in_specs=[SMEM, SMEM, VMEM, VMEM, VMEM],
         out_specs=VMEM,
-        scratch_shapes=[pltpu.VMEM((JT * TILE, 2 * TILE), BF16)] * SUB,
+        scratch_shapes=[pltpu.VMEM((JT * TILE, 2 * TILE), BF16)] * HELD,
         compiler_params=pltpu.CompilerParams(vmem_limit_bytes=40 * 2**20),
         name="apply",
     )(lists, info, xj, vj, xi)

time: 53.8 us -> 50 us (0.929)
  the two profiles are of different devices: /device:TPU:1 before, /device:TPU:8 now
where the time goes in v4:
time: 50 us; the launch traced here: 49.2 us
  Pallas kernels  48.5 us (97%)
  local copies, waits for them, and re-layouts  0.61 us (1%)
    pallas_call x1, Pallas kernels, local(): pl.pallas_call(gather_kernel, out_shape=(shape((CT + 1, TILE, TILE), BF16...  22.9 us
    pallas_call x1, Pallas kernels, local(): pl.pallas_call(apply_kernel, out_shape=shape((RT, PW, TILE), F32), in_spe...  15.8 us
    pallas_call x1, Pallas kernels, local(): pl.pallas_call(reduce_kernel, out_shape=shape((PW, BLK), F32), in_specs=[...  9.86 us

profile of v4, /device:TPU:8, one launch (start us, length us, event | category | flops | bytes accessed | tf_op | source)
XLA Modules:
  0.0 49.2 jit_solution(1130127779370154159)
XLA Ops:
  0.0 22.9 %gather.1 = (bf16[97,128,128]{2,1,0:T(8,128)(2,1)S(1)}, bf16[97,16,128]{2,1,0:T(8,128)(2,1)S(1)}, bf16[24,128,128]{2,1,0:T(8,128)(2,1)S(1)}, s32[16,128]{1,0:T(8,128)S(1)}, s32[16,128]{1,0:T(8,128)S(1)}) custom-call(bf16[64,384]{1,0:T(8,128)(2,1)} %bitcast.4, bf16[16,384]{1,0:T(8,128)(2,1)} %bitcast.5, s32[24,768]{1,0:T(8,128)} %tp.1), custom_call_target="tpu_custom_call" | custom-call | tf_op jit(solution)/shard_map/gather/pallas_call | solution.py:420
  22.9 15.8 %apply.1.part = f32[24,16,128]{2,1,0:T(8,128)S(1)} custom-call(s32[16,128]{1,0:T(8,128)S(1)} %get-tuple-element.10.lists, s32[16,128]{1,0:T(8,128)S(1)} %get-tuple-element.11.info, bf16[97,128,128]{2,1,0:T(8,128)(2,1)S(1)} %get-tuple-element.12.xj, bf16[97,16,128]{2,1,0:T(8,128)(2,1)S(1)} %get-tuple-element.13.vj, bf16[24,128,128]{2,1,0:T(8,128)(2,1)S(1)} %get-tuple-element.14.xi), custom_call_target="tpu_custom_call" | custom-call | tf_op jit(solution)/shard_map/apply/pallas_call | solution.py:456
  38.7 9.9 %reduce.1 = f32[16,384]{1,0:T(8,128)S(1)} custom-call(f32[24,16,128]{2,1,0:T(8,128)S(1)} %apply.1.part, bf16[97,128,128]{2,1,0:T(8,128)(2,1)S(1)} %get-tuple-element.12.xj, bf16[97,16,128]{2,1,0:T(8,128)(2,1)S(1)} %get-tuple-element.13.vj, bf16[24,128,128]{2,1,0:T(8,128)(2,1)S(1)} %get-tuple-element.14.xi), custom_call_target="tpu_custom_call" | custom-call | tf_op jit(solution)/shard_map/reduce/pallas_call | solution.py:465
  48.6 0.6 %copy.5 = f32[384,16]{0,1:T(8,128)} copy(f32[384,16]{0,1:T(8,128)S(1)} %bitcast.3) | data formatting | bytes 49152

commit v5 on v4

--- a/solution.py
+++ b/solution.py
@@ -112,7 +112,7 @@
 
 def gather_kernel(
     pts, pan, tp, xj, vj, xi, lists, info,
-    own, pairs, colbuf, rowbuf, flags, flagbuf, up, down, mask, local, psend, precv, fsend, frecv, zsend, zrecv, gsend, grecv,
+    own, pairs, colbuf, rowbuf, flags, flagbuf, up, down, mask, away, local, psend, precv, fsend, frecv, zsend, zrecv, gsend, grecv,
 ):
     x, y, z, core = place()
     c = (x // 2) * 4 + y
@@ -144,8 +144,8 @@
     for copy in fetch:
         copy.wait()
     r, t = iota((16, 24), 0), iota((16, 24), 1)
-    pick = jnp.where((r < 3) & (t == 3 * c + r), 1.0, 0.0)
-    rows = jnp.dot(pick, pairs[...].astype(F32), preferred_element_type=F32)
+    pick = jnp.where((r < 3) & (t == 3 * c + r), 1.0, 0.0).astype(BF16)
+    rows = jnp.dot(pick, pairs[...].astype(BF16), preferred_element_type=F32)
     for zz in range(NZ):
         low = rows[:, 48 * zz : 48 * zz + 48]
         high = rows[:, BLK + 48 * zz : BLK + 48 * zz + 48]
@@ -217,12 +217,10 @@
         for q in range(3):
             cut = slice(q * TILE, (q + 1) * TILE)
             tail = mix(row64[0:8], 3, hi[:, cut], mid[:, cut], lo[:, cut], 0)
-            on = jnp.sum(jnp.where(lanes == 3 * s + q, mask[...], 0.0), axis=1, keepdims=True)
-            off = jnp.broadcast_to((on - 1.0) * BIG, (RT, TILE))
-            feats = jnp.concatenate(
-                [block[0:D, cut].astype(F32), tail, off, jnp.zeros((128 - D - 8 - RT, TILE), F32)], axis=0
-            )
-            xj[3 * s + q] = feats.T.astype(BF16)
+            off = jnp.sum(jnp.where(lanes == 3 * s + q, away[...], 0.0), axis=1, keepdims=True)
+            off = jnp.broadcast_to(off, (RT, TILE))
+            tail = jnp.concatenate([tail, off, jnp.zeros((128 - D - 8 - RT, TILE), F32)], axis=0)
+            xj[3 * s + q] = jnp.concatenate([block[0:D, cut], tail.astype(BF16)], axis=0).T
             vj[3 * s + q] = block[D:, cut]
 
     xj[CT] = jnp.zeros((TILE, TILE), BF16)
@@ -274,6 +272,7 @@
     flagbuf[above] = down[1]
     for zz in range(NZ):
         mask[3 * zz : 3 * zz + 3, :] = flagbuf[zz].astype(F32)[0:3, :]
+    away[...] = (mask[...] - 1.0) * BIG
     column(me, own[...])
     for d in two + side + diagonal:
         column(slot(d), colbuf[slot(d)])
@@ -362,7 +361,7 @@
 def reduce_kernel(part, xj, vj, xi, out, got, held, total, send, recv):
     x, y, z, core = place()
     barrier = pltpu.get_barrier_semaphore()
-    for o in range(1, NZ):
+    for o in (4, 3, 5, 2, 6, 1, 7):
         pl.semaphore_signal(barrier, inc=1, device_id=device(x, y, (z + o) % NZ, core), device_id_type=MESH)
     pl.semaphore_wait(barrier, NZ - 1)
 
@@ -437,6 +436,7 @@
             pltpu.VMEM((NZ, 16, 128), BF16),
             pltpu.VMEM((3, 16, 128), BF16),
             pltpu.VMEM((2, 16, 128), BF16),
+            pltpu.VMEM((RT, 128), F32),
             pltpu.VMEM((RT, 128), F32),
             dma((3,)),
             dma((16,)),

time: 50 us -> 49.5 us (0.990)
  no operation moved by 1% of the time
where the time goes in v5:
time: 49.5 us; the launch traced here: 49 us
  Pallas kernels  48.3 us (98%)
  local copies, waits for them, and re-layouts  0.61 us (1%)
    pallas_call x1, Pallas kernels, local(): pl.pallas_call(gather_kernel, out_shape=(shape((CT + 1, TILE, TILE), BF16...  22.5 us
    pallas_call x1, Pallas kernels, local(): pl.pallas_call(apply_kernel, out_shape=shape((RT, PW, TILE), F32), in_spe...  15.8 us
    pallas_call x1, Pallas kernels, local(): pl.pallas_call(reduce_kernel, out_shape=shape((PW, BLK), F32), in_specs=[...  10.1 us

profile of v5, /device:TPU:8, one launch (start us, length us, event | category | flops | bytes accessed | tf_op | source)
XLA Modules:
  0.0 49.0 jit_solution(13777780237934497743)
XLA Ops:
  0.0 22.5 %gather.1 = (bf16[97,128,128]{2,1,0:T(8,128)(2,1)S(1)}, bf16[97,16,128]{2,1,0:T(8,128)(2,1)S(1)}, bf16[24,128,128]{2,1,0:T(8,128)(2,1)S(1)}, s32[16,128]{1,0:T(8,128)S(1)}, s32[16,128]{1,0:T(8,128)S(1)}) custom-call(bf16[64,384]{1,0:T(8,128)(2,1)} %bitcast.4, bf16[16,384]{1,0:T(8,128)(2,1)} %bitcast.5, s32[24,768]{1,0:T(8,128)} %tp.1), custom_call_target="tpu_custom_call" | custom-call | tf_op jit(solution)/shard_map/gather/pallas_call | solution.py:419
  22.5 15.8 %apply.1.part = f32[24,16,128]{2,1,0:T(8,128)S(1)} custom-call(s32[16,128]{1,0:T(8,128)S(1)} %get-tuple-element.10.lists, s32[16,128]{1,0:T(8,128)S(1)} %get-tuple-element.11.info, bf16[97,128,128]{2,1,0:T(8,128)(2,1)S(1)} %get-tuple-element.12.xj, bf16[97,16,128]{2,1,0:T(8,128)(2,1)S(1)} %get-tuple-element.13.vj, bf16[24,128,128]{2,1,0:T(8,128)(2,1)S(1)} %get-tuple-element.14.xi), custom_call_target="tpu_custom_call" | custom-call | tf_op jit(solution)/shard_map/apply/pallas_call | solution.py:456
  38.3 10.1 %reduce.1 = f32[16,384]{1,0:T(8,128)S(1)} custom-call(f32[24,16,128]{2,1,0:T(8,128)S(1)} %apply.1.part, bf16[97,128,128]{2,1,0:T(8,128)(2,1)S(1)} %get-tuple-element.12.xj, bf16[97,16,128]{2,1,0:T(8,128)(2,1)S(1)} %get-tuple-element.13.vj, bf16[24,128,128]{2,1,0:T(8,128)(2,1)S(1)} %get-tuple-element.14.xi), custom_call_target="tpu_custom_call" | custom-call | tf_op jit(solution)/shard_map/reduce/pallas_call | solution.py:465
  48.4 0.6 %copy.5 = f32[384,16]{0,1:T(8,128)} copy(f32[384,16]{0,1:T(8,128)S(1)} %bitcast.3) | data formatting | bytes 49152
